TPU v7x, 512 devices: a whole 4x8x8 slice. The times are simulated.
512 devices in a mesh: grp: 16 (over z, core), dev: 32 (over y, x).
Axes of the slice: x: 4, y: 8, z: 8, core: 2. Of those that a mesh axis runs over, the one named last changes fastest.
Arguments:
- amplitudes: bfloat16 [1024, 256, 256], P(('grp', 'dev')), may hold values from -6 to 6
- integrals: bfloat16 [1024, 256, 256], P(('grp', 'dev')), may hold values from -6 to 6
- virt_energy: float32 [1024, 256], P(('grp', 'dev')), may hold values from 0.2 to 2
- pair_gap: float32 [1024], P(('grp', 'dev')), may hold values from 0.3 to 1.5
- rank_bucket: int32 [1024], P('grp'), may hold values from 0 to 3
- neighbours: int32 [1024, 8], P('grp'), may hold values from 0 to 63, as said below
- intersection: bfloat16 [1024, 8, 256, 256], P(('grp', 'dev')), may hold values from -0.375 to 0.375
- coupling: float32 [1024, 8], P(('grp', 'dev')), may hold values from -3 to 3
- edge_local: int32 [1024, 2], P(('grp', 'dev')), may hold values from 0 to 1
- edge_intersection: bfloat16 [1024, 2, 256, 256], P(('grp', 'dev')), may hold values from -0.375 to 0.375
- edge_coupling: float32 [1024, 2], P(('grp', 'dev')), may hold values from -3 to 3
Outputs:
- residual: float32 [1024, 256, 256], P(('grp', 'dev'))
- new_amplitudes: bfloat16 [1024, 256, 256], P(('grp', 'dev'))
Inputs may be any that keep to these rules, and one draw needn't show every extreme that they name: `neighbours`: pair number n of a group is held by device n // 2 of that group. Among the 16 entries of the pairs of one device, at most 1 name pairs held by any one device; in each group some device is named exactly 1 times by the entries of every device of the group.
All inputs are finite; a program needn't handle non-finite values.
Results may differ from a plain program's by a relative error of at most 0.0049.
Values may be sent and summed in bfloat16 or wider, within the bound.
No kernel may reach another device: no remote copies, remote signals or barrier semaphores. Data moves between devices by JAX's collectives and lax.ppermute only.
A program may use at most 128 MiB of HBM per device.

v0:
```python
import jax
import jax.numpy as jnp
from jax import lax
from jax.sharding import PartitionSpec as P


def padded(cells, sides, width):
    for axis, dim in sides:
        count = lax.axis_size(axis)
        ends = count - 1
        head = lax.slice_in_dim(cells, 0, width, axis=dim)
        tail = lax.slice_in_dim(cells, cells.shape[dim] - width, cells.shape[dim], axis=dim)
        cells = jnp.concatenate(
            [
                lax.ppermute(tail, axis, [(i, (i + 1) % count) for i in range(ends)]),
                cells,
                lax.ppermute(head, axis, [((i + 1) % count, i) for i in range(ends)]),
            ],
            axis=dim,
        )
    return cells


def local(
    amplitudes,
    integrals,
    virt_energy,
    pair_gap,
    rank_bucket,
    neighbours,
    intersection,
    coupling,
    edge_local,
    edge_intersection,
    edge_coupling,
):
    pair_count = amplitudes.shape[0]
    rank_width = amplitudes.shape[1]
    nbr_count = neighbours.shape[1]
    slot_count = pair_count * nbr_count
    devices = lax.axis_size("dev")
    capacity = (slot_count + devices - 1) // devices
    my_index = lax.axis_index("dev")
    positions = jnp.arange(rank_width, dtype=jnp.int32)
    bucket_own = lax.dynamic_slice_in_dim(rank_bucket, my_index * pair_count, pair_count)
    rank_own = rank_width // 8 * jnp.left_shift(jnp.ones_like(bucket_own), bucket_own)
    keep_rows = positions[None, :] < rank_own[:, None]
    keep_square = keep_rows[:, :, None] & keep_rows[:, None, :]
    masked = jnp.where(keep_square, amplitudes, jnp.zeros_like(amplitudes))
    row_masked = jnp.where(
        keep_rows[:, None, :, None], intersection, jnp.zeros_like(intersection)
    ).reshape(slot_count, rank_width, rank_width)
    edge_rows = jnp.where(
        keep_rows[:, None, :, None], edge_intersection, jnp.zeros_like(edge_intersection)
    )
    own_nbrs = lax.dynamic_slice_in_dim(neighbours, my_index * pair_count, pair_count, 0).reshape(
        slot_count
    )
    own_owner = own_nbrs // pair_count
    slot_ids = jnp.arange(slot_count, dtype=jnp.int32)
    same_owner = own_owner[:, None] == own_owner[None, :]
    earlier = slot_ids[None, :] < slot_ids[:, None]
    own_order = jnp.sum((same_owner & earlier).astype(jnp.int32), axis=1)
    own_place = own_owner * capacity + own_order
    group_nbrs = neighbours.reshape(devices, slot_count)
    asked = group_nbrs // pair_count == my_index
    asked_order = jnp.cumsum(asked.astype(jnp.int32), axis=1) - 1
    selector = asked[:, None, :] & (
        asked_order[:, None, :] == jnp.arange(capacity, dtype=jnp.int32)[None, :, None]
    )
    served_pair = jnp.sum(
        jnp.where(selector, (group_nbrs % pair_count)[:, None, :], 0), axis=2
    ).reshape(devices * capacity)
    served_live = jnp.any(selector, axis=2).reshape(devices * capacity)
    beside_all = padded(masked, (("grp", 0),), pair_count)
    shard_rows = lax.all_gather(masked, "dev", axis=0, tiled=True)
    picker = (
        own_nbrs[:, None] == jnp.arange(shard_rows.shape[0], dtype=jnp.int32)[None, :]
    ).astype(jnp.bfloat16)
    added = jnp.einsum("sn,nab->sab", picker, shard_rows, preferred_element_type=jnp.float32)
    partner = added.astype(jnp.bfloat16)
    half_in = jnp.einsum(
        "sab,sbc->sac", row_masked, partner, preferred_element_type=jnp.float32
    ).astype(jnp.bfloat16)
    projected = jnp.einsum("sac,sdc->sad", half_in, row_masked, preferred_element_type=jnp.float32)
    grouped = row_masked.reshape(pair_count, nbr_count, rank_width, rank_width)
    half_out = jnp.einsum(
        "pnba,pbc->pnac", grouped, masked, preferred_element_type=jnp.float32
    ).astype(jnp.bfloat16)
    returned = jnp.einsum(
        "pnac,pncd->pnad", half_out, grouped, preferred_element_type=jnp.float32
    ).reshape(slot_count, rank_width, rank_width)
    weights_flat = coupling.reshape(slot_count)
    contributions = (weights_flat[:, None, None] * returned).astype(jnp.bfloat16)
    outgoing_back = (
        jnp.zeros((devices * capacity, rank_width, rank_width), jnp.bfloat16)
        .at[own_place]
        .set(contributions)
    )
    arrived_back = lax.all_to_all(
        outgoing_back.reshape(devices, capacity, rank_width, rank_width),
        "dev",
        split_axis=0,
        concat_axis=0,
        tiled=True,
    )
    gather_rows = (
        (served_pair[None, :] == jnp.arange(pair_count, dtype=jnp.int32)[:, None])
        & served_live[None, :]
    ).astype(jnp.bfloat16)
    gathered = jnp.einsum(
        "pk,kab->pab",
        gather_rows,
        arrived_back.reshape(devices * capacity, rank_width, rank_width),
        preferred_element_type=jnp.float32,
    )
    local_sum = jnp.sum(
        (weights_flat[:, None, None] * projected).reshape(
            pair_count, nbr_count, rank_width, rank_width
        ),
        axis=1,
    )
    lower_amps = jnp.take(beside_all, edge_local[:, 0], axis=0)
    upper_amps = jnp.take(beside_all, 2 * pair_count + edge_local[:, 1], axis=0)
    edge_partner = jnp.stack([lower_amps, upper_amps], axis=1)
    edge_half = jnp.einsum(
        "pnab,pnbc->pnac", edge_rows, edge_partner, preferred_element_type=jnp.float32
    ).astype(jnp.bfloat16)
    edge_proj = jnp.einsum(
        "pnac,pndc->pnad", edge_half, edge_rows, preferred_element_type=jnp.float32
    )
    edge_sum = jnp.sum(edge_coupling[:, :, None, None] * edge_proj, axis=1)
    denom = virt_energy[:, :, None] + virt_energy[:, None, :] + pair_gap[:, None, None]
    residual = jnp.where(
        keep_square,
        integrals.astype(jnp.float32)
        + denom * masked.astype(jnp.float32)
        - local_sum
        - edge_sum
        - gathered,
        jnp.float32(0.0),
    )
    new_amplitudes = jnp.where(
        keep_square, masked.astype(jnp.float32) - residual / denom, jnp.float32(0.0)
    ).astype(jnp.bfloat16)
    return (residual, new_amplitudes)


def solution(mesh):
    placed = (
        P(("grp", "dev"), None, None),
        P(("grp", "dev"), None, None),
        P(("grp", "dev"), None),
        P(("grp", "dev")),
        P("grp"),
        P("grp", None),
        P(("grp", "dev"), None, None, None),
        P(("grp", "dev"), None),
        P(("grp", "dev"), None),
        P(("grp", "dev"), None, None, None),
        P(("grp", "dev"), None),
    )
    return jax.shard_map(
        local,
        mesh=mesh,
        in_specs=placed,
        out_specs=(P(("grp", "dev"), None, None), P(("grp", "dev"), None, None)),
        check_vma=False,
    )
```

profile of v0, /device:TPU:1, one launch (start us, length us, event | category | flops | bytes accessed | tf_op | source)
XLA Modules:
  0.0 212.5 jit_solution(11519641661761994297)
XLA Ops:
  7.2 0.7 shift-left_multiply_fusion
  8.2 1.5 and_select_fusion.2
  9.7 0.7 copy.62
  10.5 0.8 constant_dynamic-slice_fusion
  11.5 0.8 mul.37
  12.5 1.5 fusion.79
  14.0 1.8 broadcast_select_fusion
  15.8 3.3 %fusion.8 = f32[2,8,256,256]{3,2,1,0:T(8,128)} fusion(bf16[2,8,256,256]{3,2,1,0:T(8,128)(2,1)S(1)} %broadcast_select_fusion, bf16[2,256,256,1]{2,0,1,3:T(2,128)(2,1)S(1)} %fusion.79), kind=kOutput, calls=%fused_computation.14 | convolution fusion | flops 1074790400 | bytes 6553600 | tf_op jit(solution)/shard_map/pnac,pncd->pnad/dot_general | solution.py:90
  19.1 4.0 %fusion.4 = bf16[16,256,256]{2,1,0:T(8,128)(2,1)} fusion(f32[2,8,256,256]{3,2,1,0:T(8,128)} %fusion.8, f32[16]{0:T(128)S(1)} %mul.37), kind=kLoop, calls=%fused_computation.8 | loop fusion | flops 2097152 | bytes 6291520 | tf_op jit(solution)/shard_map/convert_element_type | solution.py:94
  23.1 2.4 %broadcast_in_dim.44 = bf16[32,256,256]{2,1,0:T(8,128)(2,1)} broadcast(bf16[]{:T(256)} %constant.69.clone.1), dimensions={} | broadcast | bytes 4194306 | tf_op jit(solution)/shard_map/broadcast_in_dim | solution.py:96
  25.5 6.0 %scatter_fusion = bf16[32,256,256]{2,1,0:T(8,128)(2,1)} fusion(bf16[32,256,256]{2,1,0:T(8,128)(2,1)} %broadcast_in_dim.44, s32[16]{0:T(128)S(1)} %fusion.68, bf16[16,256,256]{2,1,0:T(8,128)(2,1)} %fusion.4), kind=kCustom, calls=%fused_computation.2 | custom fusion | bytes 6291520 | tf_op jit(solution)/shard_map/scatter | solution.py:98
  31.5 10.7 %all-to-all-start = ((bf16[32,1,256,256]{3,2,1,0:T(8,128)(2,1)}), bf16[32,1,256,256]{3,2,1,0:T(8,128)(2,1)}, u32[]{:S(2)}, u32[]{:S(2)}) async-start(bf16[32,1,256,256]{3,2,1,0:T(8,128)(2,1)} %bitcast.49), calls=%async_computation | async-start | bytes 8388608 | tf_op jit(solution)/shard_map/all_to_all | solution.py:100
  42.3 3.1 %collective-permute-start.1 = (bf16[2,256,256]{2,0,1:T(2,128)(2,1)S(1)}, bf16[2,256,256]{2,0,1:T(2,128)(2,1)S(1)}, u32[]{:S(2)}, u32[]{:S(2)}) collective-permute-start(bf16[2,256,256]{2,0,1:T(2,128)(2,1)S(1)} %and_select_fusion.2), channel_id=1, source_target_pairs={{32,0},{64,32},{96,64},{128,96},{160,128},{192,160},{224,192},{256... | collective-permute-start | bytes 786440 | tf_op jit(solution)/shard_map/ppermute | solution.py:17
  45.4 4.0 %collective-permute-start = (bf16[2,256,256]{2,0,1:T(2,128)(2,1)S(1)}, bf16[2,256,256]{2,0,1:T(2,128)(2,1)S(1)}, u32[]{:S(2)}, u32[]{:S(2)}) collective-permute-start(bf16[2,256,256]{2,0,1:T(2,128)(2,1)S(1)} %and_select_fusion.2), channel_id=1, source_target_pairs={{0,32},{32,64},{64,96},{96,128},{128,160},{160,192},{192,224},{224... | collective-permute-start | bytes 786440 | tf_op jit(solution)/shard_map/ppermute | solution.py:15
  50.1 0.8 copy.59
  51.7 0.8 collective-permute-done
  52.5 0.8 pad_maximum_fusion
  54.8 2.6 %fusion.24 = f32[2,256,256]{2,1,0:T(8,128)} fusion(bf16[2,1,256,256]{3,2,1,0:T(8,128)(2,1)S(1)} %select_bitcast_fusion, bf16[2,1,256,256]{3,2,1,0:T(8,128)(2,1)S(1)} %select_bitcast_fusion.1, bf16[2,2,256,256]{3,2,1,0:T(8,128)(2,1)} %param.22, f32[2,2]{1,0:T(2,128)S(1)} %copy-done.6, pred[2,256]{1,0:T(4,128)(4,1)S(1)} %iota_compare_fusion.2), kind=kOutput, calls=%fused_computation.22 | convolution fusion | flops 269877248 | bytes 1573392 | tf_op jit(solution)/shard_map/pnac,pndc->pnad/dot_general | solution.py:129
  57.4 124.7 %all-gather.2.cloned.1.call-done = bf16[64,256,256]{2,1,0:T(8,128)(2,1)} async-done(((bf16[2,256,256]{2,1,0:T(8,128)(2,1)}), bf16[64,256,256]{2,1,0:T(8,128)(2,1)}) %all-gather.2.cloned.1.call-update) | async-done | bytes 8388624 | tf_op jit(solution)/shard_map/all_gather | solution.py:76
  182.1 9.4 %fusion.17 = bf16[16,256,256]{2,0,1:T(8,128)(2,1)} fusion(bf16[64,256,256]{2,1,0:T(8,128)(2,1)} %all-gather.2.cloned.1.call-done, s32[16]{0:T(128)S(1)} %eq.83), kind=kOutput, calls=%fused_computation.19 | convolution fusion | flops 135267328 | bytes 10485824 | tf_op jit(solution)/shard_map/sn,nab->sab/dot_general | solution.py:80
  191.4 4.0 %bitcast_reduce_fusion = f32[2,256,256]{2,1,0:T(8,128)} fusion(bf16[16,256,256]{2,1,0:T(8,128)(2,1)S(1)} %bitcast.50, bf16[16,256,256]{2,0,1:T(8,128)(2,1)} %fusion.17, f32[16]{0:T(128)S(1)} %mul.37), kind=kOutput, calls=%fused_computation.9 | convolution fusion | flops 1076756480 | bytes 4718656 | tf_op jit(solution)/shard_map/sac,sdc->sad/dot_general | solution.py:85
  195.5 8.6 %fusion.33 = (bf16[2,256,256]{2,0,1:T(2,128)(2,1)S(1)}, f32[2,256,256]{2,0,1:T(2,128)S(1)}) fusion(pred[2,256]{1,0:T(4,128)(4,1)S(1)} %iota_compare_fusion.2, pred[2,256]{0,1:T(8,128)(4,1)S(1)} %copy.57, f32[2]{0:T(128)S(1)} %copy-done.7, f32[2,256]{1,0:T(2,128)S(1)} %copy-done.4, f32[2,256]{0,1:T(8,128)S(1)} %copy-done.1, ...), kind=kOutput, calls=%fused_computation.33 | convolution fusion | flops 10616960 | bytes 6558888 | tf_op jit(solution)/shard_map/pk,kab->pab/dot_general | solution.py:111
  204.1 0.7 copy.77
  204.8 0.8 copy.76
  (45 shorter events, 3.8 us)
Async XLA Ops:
  7.2 174.9 %all-gather.2.cloned.1.call-start = ((), (), s32[]{:S(2)}) async-start(), calls=%async_computation.1 | async-start | bytes 8650752 | tf_op jit(solution)/shard_map/all_gather | solution.py:76
  31.5 17.9 %copy-start.2 = (s32[64,8]{0,1:T(8,128)S(1)}, s32[64,8]{0,1:T(8,128)}, u32[]{:S(2)}) copy-start(s32[64,8]{0,1:T(8,128)} %param.18) | copy-start | bytes 6148
  31.5 18.3 %copy-start.3 = (s32[2,2]{1,0:T(2,128)S(1)}, s32[2,2]{1,0:T(2,128)}, u32[]{:S(2)}) copy-start(s32[2,2]{1,0:T(2,128)} %param.21) | copy-start | bytes 52
  31.5 18.6 %copy-start.4 = (f32[2,256]{1,0:T(2,128)S(1)}, f32[2,256]{1,0:T(2,128)}, u32[]{:S(2)}) copy-start(f32[2,256]{1,0:T(2,128)} %param.15) | copy-start | bytes 6148
  31.5 164.0 %all-to-all-start = ((bf16[32,1,256,256]{3,2,1,0:T(8,128)(2,1)}), bf16[32,1,256,256]{3,2,1,0:T(8,128)(2,1)}, u32[]{:S(2)}, u32[]{:S(2)}) async-start(bf16[32,1,256,256]{3,2,1,0:T(8,128)(2,1)} %bitcast.49), calls=%async_computation | async-start | bytes 8388608 | tf_op jit(solution)/shard_map/all_to_all | solution.py:100
  42.3 9.4 %collective-permute-start.1 = (bf16[2,256,256]{2,0,1:T(2,128)(2,1)S(1)}, bf16[2,256,256]{2,0,1:T(2,128)(2,1)S(1)}, u32[]{:S(2)}, u32[]{:S(2)}) collective-permute-start(bf16[2,256,256]{2,0,1:T(2,128)(2,1)S(1)} %and_select_fusion.2), channel_id=1, source_target_pairs={{32,0},{64,32},{96,64},{128,96},{160,128},{192,160},{224,192},{256... | collective-permute-start | bytes 786440 | tf_op jit(solution)/shard_map/ppermute | solution.py:17
  45.4 7.1 %collective-permute-start = (bf16[2,256,256]{2,0,1:T(2,128)(2,1)S(1)}, bf16[2,256,256]{2,0,1:T(2,128)(2,1)S(1)}, u32[]{:S(2)}, u32[]{:S(2)}) collective-permute-start(bf16[2,256,256]{2,0,1:T(2,128)(2,1)S(1)} %and_select_fusion.2), channel_id=1, source_target_pairs={{0,32},{32,64},{64,96},{96,128},{128,160},{160,192},{192,224},{224... | collective-permute-start | bytes 786440 | tf_op jit(solution)/shard_map/ppermute | solution.py:15
  53.3 1.5 copy-start.6
  191.4 4.0 %copy-start = (bf16[2,256,256]{2,1,0:T(8,128)(2,1)S(1)}, bf16[2,256,256]{2,1,0:T(8,128)(2,1)}, u32[]{:S(2)}) copy-start(bf16[2,256,256]{2,1,0:T(8,128)(2,1)} %param.13) | copy-start | bytes 786436
  191.4 4.0 %copy-start.1 = (f32[2,256]{0,1:T(8,128)S(1)}, f32[2,256]{0,1:T(8,128)}, u32[]{:S(2)}) copy-start(f32[2,256]{0,1:T(8,128)} %copy.59) | copy-start | bytes 6148
  191.4 4.0 %copy-start.5 = (bf16[2,256,256]{2,1,0:T(8,128)(2,1)S(1)}, bf16[2,256,256]{2,1,0:T(8,128)(2,1)}, u32[]{:S(2)}) copy-start(bf16[2,256,256]{2,1,0:T(8,128)(2,1)} %param.14) | copy-start | bytes 786436
  191.4 4.0 %copy-start.7 = (f32[2]{0:T(128)S(1)}, f32[2]{0:T(128)}, u32[]{:S(2)}) copy-start(f32[2]{0:T(128)} %param.16) | copy-start | bytes 28
Sparse Core Ops, SparseCore 0:
  11.7 170.2 all-gather.1
where the time goes:
time: 213 us
  waiting for transfers between devices  126 us (59%)
  matrix products  27.9 us (13%)
  starting transfers between devices  17.9 us (8%)
  local copies, waits for them, and re-layouts  15 us (7%)
  between operations  14.2 us (7%)
  other arithmetic  11.5 us (5%)
    all_gather x1, waiting for transfers between devices, local(): shard_rows = lax.all_gather(masked, 'dev', axis=0, tiled=True)  125 us
    all_to_all x1, starting transfers between devices, local(): lax.all_to_all(outgoing_back.reshape(devices, capacity, rank_width, rank_...  10.7 us
    dot_general x1, matrix products, local(): jnp.einsum('sn,nab->sab', picker, shard_rows, preferred_element_type=jnp....  9.36 us
    dot_general x1, matrix products, local(): jnp.einsum('pk,kab->pab', gather_rows, arrived_back.reshape(devices * cap...  8.62 us
    scatter x1, local copies, waits for them, and re-layouts, local(): outgoing_back = jnp.zeros((devices * capacity, rank_width, rank_width), j...  5.96 us
  transfers between devices with their start and end apart: 4, of which 3 were waited for; matrix products, arithmetic and copies ran while one was open for 19% of the time, Pallas kernels for 0%

commit v1 on v0

v1 whole, which is shorter than its diff:
```python
import functools

import jax
import jax.numpy as jnp
from jax import lax
from jax.experimental import pallas as pl
from jax.experimental.pallas import tpu as pltpu
from jax.sharding import PartitionSpec as P

R = 256
NBR = 8
COLS = 4
ROWS = 8
BF = jnp.bfloat16
F32 = jnp.float32
LIMIT = 56 << 20

SMEM = pl.BlockSpec(memory_space=pltpu.SMEM)
VMEM = pl.BlockSpec(memory_space=pltpu.VMEM)
ANY = pl.BlockSpec(memory_space=pl.ANY)


def place():
    dev = lax.axis_index("dev")
    return dev, dev // COLS, dev % COLS


def keep_square(rank):
    rows = lax.broadcasted_iota(jnp.int32, (R, R), 0)
    cols = lax.broadcasted_iota(jnp.int32, (R, R), 1)
    return jnp.maximum(rows, cols) < rank


def return_kernel(bucket, nbr, coupling, amps, inter, masked, out, terms, sems):
    dev, _, _ = place()
    pair = pl.program_id(0)

    def copy(pair_at, entry):
        holder = nbr[2 * dev + pair_at, entry] >> 1
        slot = (holder & (COLS - 1)) * ROWS + (holder >> 2)
        index = pair_at * NBR + entry
        return pltpu.make_async_copy(terms.at[index], out.at[slot], sems.at[index])

    rank = jnp.left_shift(32, bucket[2 * dev + pair])
    own = jnp.where(keep_square(rank), amps[0].astype(F32), 0.0).astype(BF)
    masked[0] = own
    for entry in range(NBR):
        s = inter[0, entry]
        half = lax.dot_general(s, own, (((0,), (0,)), ((), ())), preferred_element_type=F32)
        term = jnp.dot(half.astype(BF), s, preferred_element_type=F32)
        terms[pair * NBR + entry] = (coupling[pair, entry] * term).astype(BF)
    for entry in range(NBR):
        copy(pair, entry).start()

    @pl.when(pair == 1)
    def _():
        for pair_at in range(2):
            for entry in range(NBR):
                copy(pair_at, entry).wait()


def select_kernel(nbr, column, out, sems):
    _, y, x = place()

    def each(act):
        for taker_x in range(COLS):

            def body(i, _):
                name = nbr[2 * (y * COLS + taker_x) + i // NBR, i % NBR]
                holder = name >> 1

                @pl.when((holder & (COLS - 1)) == x)
                def _():
                    act(
                        pltpu.make_async_copy(
                            column.at[2 * (holder >> 2) + (name & 1)],
                            out.at[taker_x * ROWS + (holder >> 2)],
                            sems.at[taker_x, i],
                        )
                    )

                return 0

            lax.fori_loop(0, 2 * NBR, body, 0)

    each(lambda copy: copy.start())
    each(lambda copy: copy.wait())


def combine_kernel(nbr, r0, r1, r2, r3, dense, table):
    _, y, x = place()

    @pl.when(pl.program_id(0) == 0)
    def _():
        for giver_x in range(COLS):
            for row in range(ROWS):
                table[giver_x, row] = 0

            def body(i, _):
                name = nbr[2 * (y * COLS + giver_x) + i // NBR, i % NBR]
                holder = name >> 1

                @pl.when((holder & (COLS - 1)) == x)
                def _():
                    table[giver_x, holder >> 2] = 1 + (name & 1)

                return 0

            lax.fori_loop(0, 2 * NBR, body, 0)

    for j in range(2):
        row = pl.program_id(0) * 2 + j
        for chunk in range(0, R, 64):
            at = pl.ds(chunk, 64)
            vals = [ref[j, at, :].astype(F32) for ref in (r0, r1, r2, r3)]
            for local in range(2):
                total = jnp.zeros((64, R), F32)
                for giver_x in range(COLS):
                    total += jnp.where(table[giver_x, row] == 1 + local, vals[giver_x], 0.0)
                dense[2 * j + local, at, :] = total.astype(BF)


def final_kernel(
    bucket,
    nbr,
    coupling,
    edge_local,
    edge_coupling,
    gap,
    masked,
    integrals,
    virt,
    inter,
    edge_inter,
    lower,
    upper,
    gathered,
    named,
    residual,
    new_amps,
    partners,
    sems,
):
    dev, _, _ = place()

    def copy(index):
        name = nbr[2 * dev + index // NBR, index % NBR]
        holder = name >> 1
        slot = (holder & (COLS - 1)) * ROWS + (holder >> 2)
        return pltpu.make_async_copy(named.at[slot], partners.at[index], sems.at[index])

    for index in range(2 * NBR):
        copy(index).start()

    def project(s, a):
        half = jnp.dot(s, a, preferred_element_type=F32).astype(BF)
        return lax.dot_general(half, s, (((1,), (1,)), ((), ())), preferred_element_type=F32)

    for pair in range(2):
        total = edge_coupling[pair, 0] * project(
            edge_inter[pair, 0], lower[edge_local[pair, 0]]
        )
        total += edge_coupling[pair, 1] * project(
            edge_inter[pair, 1], upper[edge_local[pair, 1]]
        )
        for entry in range(NBR):
            index = pair * NBR + entry
            copy(index).wait()
            total += coupling[pair, entry] * project(inter[pair, entry], partners[index])
        energy = jnp.broadcast_to(virt[pair : pair + 1, :], (R, R))
        denom = energy + energy.T + gap[pair]
        own = masked[pair].astype(F32)
        rank = jnp.left_shift(32, bucket[2 * dev + pair])
        keep = keep_square(rank)
        value = (
            integrals[pair].astype(F32) + denom * own - total - gathered[pair].astype(F32)
        )
        value = jnp.where(keep, value, 0.0)
        residual[pair] = value
        new_amps[pair] = jnp.where(keep, own - value / denom, 0.0).astype(BF)


def local(
    amplitudes,
    integrals,
    virt_energy,
    pair_gap,
    rank_bucket,
    neighbours,
    intersection,
    coupling,
    edge_local,
    edge_intersection,
    edge_coupling,
):
    groups = lax.axis_size("grp")
    devices = lax.axis_size("dev")
    columns = [[y * COLS + x for y in range(ROWS)] for x in range(COLS)]

    rows = [[y * COLS + x for x in range(COLS)] for y in range(ROWS)]

    def swap_columns(value):
        return lax.all_to_all(value, "dev", 0, 0, tiled=True, axis_index_groups=rows)

    block = jax.ShapeDtypeStruct((COLS * ROWS, R, R), BF)
    masked, outgoing = pl.pallas_call(
        return_kernel,
        grid=(2,),
        in_specs=[
            SMEM,
            SMEM,
            SMEM,
            pl.BlockSpec((1, R, R), lambda i: (i, 0, 0)),
            pl.BlockSpec((1, NBR, R, R), lambda i: (i, 0, 0, 0)),
        ],
        out_specs=[pl.BlockSpec((1, R, R), lambda i: (i, 0, 0)), ANY],
        out_shape=[jax.ShapeDtypeStruct((2, R, R), BF), block],
        scratch_shapes=[
            pltpu.VMEM((2 * NBR, R, R), BF),
            pltpu.SemaphoreType.DMA((2 * NBR,)),
        ],
        compiler_params=pltpu.CompilerParams(vmem_limit_bytes=LIMIT),
        name="returned_terms",
    )(rank_bucket, neighbours, coupling, amplitudes, intersection)
    arrived = swap_columns(outgoing)
    lower = lax.ppermute(masked, "grp", [(i, i + 1) for i in range(groups - 1)])
    upper = lax.ppermute(masked, "grp", [(i + 1, i) for i in range(groups - 1)])
    column = lax.all_gather(masked, "dev", axis=0, tiled=True, axis_index_groups=columns)
    chosen = pl.pallas_call(
        select_kernel,
        in_specs=[SMEM, VMEM],
        out_specs=ANY,
        out_shape=block,
        scratch_shapes=[pltpu.SemaphoreType.DMA((COLS, 2 * NBR))],
        compiler_params=pltpu.CompilerParams(vmem_limit_bytes=LIMIT),
        name="named_pairs",
    )(neighbours, column)
    named = swap_columns(chosen)
    dense = pl.pallas_call(
        combine_kernel,
        grid=(4,),
        in_specs=[SMEM]
        + [
            pl.BlockSpec((2, R, R), functools.partial(lambda x, i: (x * 4 + i, 0, 0), x))
            for x in range(COLS)
        ],
        out_specs=pl.BlockSpec((4, R, R), lambda i: (i, 0, 0)),
        out_shape=jax.ShapeDtypeStruct((2 * ROWS, R, R), BF),
        scratch_shapes=[pltpu.SMEM((COLS, ROWS), jnp.int32)],
        compiler_params=pltpu.CompilerParams(vmem_limit_bytes=LIMIT),
        name="column_terms",
    )(neighbours, *[arrived] * COLS)
    gathered = lax.psum_scatter(
        dense, "dev", scatter_dimension=0, tiled=True, axis_index_groups=columns
    )
    outputs = pl.pallas_call(
        final_kernel,
        in_specs=[SMEM] * 6 + [VMEM] * 8 + [ANY],
        out_specs=[VMEM, VMEM],
        out_shape=[
            jax.ShapeDtypeStruct((2, R, R), F32),
            jax.ShapeDtypeStruct((2, R, R), BF),
        ],
        scratch_shapes=[
            pltpu.VMEM((2 * NBR, R, R), BF),
            pltpu.SemaphoreType.DMA((2 * NBR,)),
        ],
        compiler_params=pltpu.CompilerParams(vmem_limit_bytes=LIMIT),
        name="residual_update",
    )(
        rank_bucket,
        neighbours,
        coupling,
        edge_local,
        edge_coupling,
        pair_gap,
        masked,
        integrals,
        virt_energy,
        intersection,
        edge_intersection,
        lower,
        upper,
        gathered,
        named,
    )
    return tuple(outputs)


def solution(mesh):
    pair = P(("grp", "dev"))
    placed = (pair, pair, pair, pair, P("grp"), P("grp")) + (pair,) * 5
    return jax.shard_map(
        local, mesh=mesh, in_specs=placed, out_specs=(pair, pair), check_vma=False
    )
```

time: 213 us -> 149 us (0.70)
  the two profiles are of different devices: /device:TPU:1 before, /device:TPU:72 now
where the time goes in v1:
time: 149 us
  blocking collectives  54.8 us (37%)
  waiting for transfers between devices  42.5 us (29%)
  Pallas kernels  25.3 us (17%)
  between operations  14.1 us (9%)
  starting transfers between devices  10.6 us (7%)
    all_to_all x1, blocking collectives, swap_columns(): lax.all_to_all(value, 'dev', 0, 0, tiled=True, axis_index_groups=rows)  54.8 us
    all_to_all x1, waiting for transfers between devices, swap_columns(): lax.all_to_all(value, 'dev', 0, 0, tiled=True, axis_index_groups=rows)  38.6 us
    pallas_call x1, Pallas kernels, local(): pl.pallas_call(final_kernel, in_specs=[SMEM] * 6 + [VMEM] * 8 + [ANY], ou...  9.7 us
    pallas_call x1, Pallas kernels, local(): pl.pallas_call(combine_kernel, grid=(4,), in_specs=[SMEM] + [pl.BlockSpec...  6.15 us
    all_to_all x1, starting transfers between devices, swap_columns(): lax.all_to_all(value, 'dev', 0, 0, tiled=True, axis_index_groups=rows)  4.98 us
    pallas_call x1, Pallas kernels, local(): pl.pallas_call(return_kernel, grid=(2,), in_specs=[SMEM, SMEM, SMEM, pl.B...  4.87 us
    pallas_call x1, Pallas kernels, local(): pl.pallas_call(select_kernel, in_specs=[SMEM, VMEM], out_specs=ANY, out_s...  4.61 us
    ppermute x1, starting transfers between devices, local(): upper = lax.ppermute(masked, 'grp', [(i + 1, i) for i in range(groups - 1)])  3.64 us
  transfers between devices with their start and end apart: 5, of which 3 were waited for; matrix products, arithmetic and copies ran while one was open for 0% of the time, Pallas kernels for 7%

profile of v1, /device:TPU:72, one launch (start us, length us, event | category | flops | bytes accessed | tf_op | source)
XLA Modules:
  0.0 148.8 jit_solution(17243682311358281075)
XLA Ops:
  7.2 0.0 all-gather.2.cloned.1.call-start
  7.2 1.4 copy.20.nbr
  8.6 4.9 %returned_terms.1 = (bf16[2,256,256]{2,1,0:T(8,128)(2,1)}, bf16[32,256,256]{2,1,0:T(8,128)(2,1)}) custom-call(s32[64]{0:T(128)} %bucket.3, s32[64,8]{1,0:T(8,128)} %copy.20.nbr, f32[2,8]{1,0:T(2,128)} %coupling.3, bf16[2,256,256]{2,1,0:T(8,128)(2,1)} %amps.1, bf16[2,8,256,256]{3,2,1,0:T(8,128)(2,1)} %inter.3), custom_call_target="tpu_custom_call" | custom-call | tf_op jit(solution)/shard_map/returned_terms/pallas_call | solution.py:206
  13.5 0.0 all-gather.2.cloned.1.call-update
  13.5 0.0 reduce-scatter.2.cloned.1.call-start
  13.5 54.8 %all_to_all.10.r0.r1.r2.r3 = bf16[32,256,256]{2,1,0:T(8,128)(2,1)} all-to-all(bf16[32,256,256]{2,1,0:T(8,128)(2,1)} %get-tuple-element.5), channel_id=1, replica_groups={{0,1,2,3},{4,5,6,7},{8,9,10,11},{12,13,14,15},{16,17,18,19},{20,21,22,2..., dimensions={0} | all-to-all | bytes 8388608 | tf_op jit(solution)/shard_map/all_to_all | solution.py:203
  68.4 6.2 %column_terms.1 = bf16[16,256,256]{2,1,0:T(8,128)(2,1)} custom-call(s32[64,8]{1,0:T(8,128)} %copy.20.nbr, bf16[32,256,256]{2,1,0:T(8,128)(2,1)} %all_to_all.10.r0.r1.r2.r3, bf16[32,256,256]{2,1,0:T(8,128)(2,1)} %all_to_all.10.r0.r1.r2.r3, bf16[32,256,256]{2,1,0:T(8,128)(2,1)} %all_to_all.10.r0.r1.r2.r3, bf16[32,256,256]{2,1,0:T(8,128)(2,1)} %all_to_all.10.r0.r1.r2.r3), custom_call_target="tpu_custom_call" | custom-call | tf_op jit(solution)/shard_map/column_terms/pallas_call | solution.py:239
  74.5 0.0 reduce-scatter.2.cloned.1.call-update
  74.6 0.0 all-gather.2.cloned.1.call-done.column
  74.6 4.6 %named_pairs.1 = bf16[32,256,256]{2,1,0:T(8,128)(2,1)} custom-call(s32[64,8]{1,0:T(8,128)} %copy.20.nbr, bf16[16,256,256]{2,1,0:T(8,128)(2,1)} %all-gather.2.cloned.1.call-done.column), custom_call_target="tpu_custom_call" | custom-call | tf_op jit(solution)/shard_map/named_pairs/pallas_call | solution.py:229
  79.2 0.0 copy-start
  79.2 5.0 %all-to-all-start.1 = ((bf16[32,256,256]{2,1,0:T(8,128)(2,1)}), bf16[32,256,256]{2,1,0:T(8,128)(2,1)}, u32[]{:S(2)}, u32[]{:S(2)}) async-start(bf16[32,256,256]{2,1,0:T(8,128)(2,1)} %named_pairs.1), calls=%async_computation.2 | async-start | bytes 8388608 | tf_op jit(solution)/shard_map/all_to_all | solution.py:203
  84.2 0.0 copy-done
  84.2 1.9 %collective-permute-start = (bf16[2,256,256]{2,1,0:T(8,128)(2,1)S(1)}, bf16[2,256,256]{2,1,0:T(8,128)(2,1)S(1)}, u32[]{:S(2)}, u32[]{:S(2)}) collective-permute-start(bf16[2,256,256]{2,1,0:T(8,128)(2,1)S(1)} %copy-done), channel_id=1, source_target_pairs={{0,32},{32,64},{64,96},{96,128},{128,160},{160,192},{192,224},{224... | collective-permute-start | bytes 786440 | tf_op jit(solution)/shard_map/ppermute | solution.py:226
  86.1 3.6 %collective-permute-start.1 = (bf16[2,256,256]{2,1,0:T(8,128)(2,1)S(1)}, bf16[2,256,256]{2,1,0:T(8,128)(2,1)S(1)}, u32[]{:S(2)}, u32[]{:S(2)}) collective-permute-start(bf16[2,256,256]{2,1,0:T(8,128)(2,1)S(1)} %copy-done), channel_id=1, source_target_pairs={{32,0},{64,32},{96,64},{128,96},{160,128},{192,160},{224,192},{256... | collective-permute-start | bytes 786440 | tf_op jit(solution)/shard_map/ppermute | solution.py:227
  89.8 2.1 %collective-permute-done.lower = bf16[2,256,256]{2,1,0:T(8,128)(2,1)S(1)} collective-permute-done((bf16[2,256,256]{2,1,0:T(8,128)(2,1)S(1)}, bf16[2,256,256]{2,1,0:T(8,128)(2,1)S(1)}, u32[]{:S(2)}, u32[]{:S(2)}) %collective-permute-start) | collective-permute-done | bytes 262176 | tf_op jit(solution)/shard_map/ppermute | solution.py:226
  91.9 0.0 copy-start.1
  91.9 1.8 %collective-permute-done.1.upper = bf16[2,256,256]{2,1,0:T(8,128)(2,1)S(1)} collective-permute-done((bf16[2,256,256]{2,1,0:T(8,128)(2,1)S(1)}, bf16[2,256,256]{2,1,0:T(8,128)(2,1)S(1)}, u32[]{:S(2)}, u32[]{:S(2)}) %collective-permute-start.1) | collective-permute-done | bytes 262176 | tf_op jit(solution)/shard_map/ppermute | solution.py:227
  93.7 0.0 copy-start.2
  93.7 38.6 %all-to-all-done.1.named = bf16[32,256,256]{2,1,0:T(8,128)(2,1)} async-done(((bf16[32,256,256]{2,1,0:T(8,128)(2,1)}), bf16[32,256,256]{2,1,0:T(8,128)(2,1)}, u32[]{:S(2)}, u32[]{:S(2)}) %all-to-all-start.1) | async-done | bytes 4194336 | tf_op jit(solution)/shard_map/all_to_all | solution.py:203
  132.3 0.0 reduce-scatter.2.cloned.1.call-done.gathered
  132.3 0.0 copy-done.1
  132.3 0.0 copy-done.2
  132.3 9.7 %residual_update.1 = (f32[2,256,256]{2,1,0:T(8,128)}, bf16[2,256,256]{2,1,0:T(8,128)(2,1)}) custom-call(s32[64]{0:T(128)} %bucket.3, s32[64,8]{1,0:T(8,128)} %copy.20.nbr, f32[2,8]{1,0:T(2,128)} %coupling.3, s32[2,2]{1,0:T(2,128)} %edge_local.1, f32[2,2]{1,0:T(2,128)} %edge_coupling.1, f32[2]{0:T(128)} %gap.1, bf16[2,256,256]{2,1,0:T(8,128)(2,1)} %get-tuple-element.4.masked, ...), custom_call_target="tpu_custom_call" | custom-call | tf_op jit(solution)/shard_map/residual_update/pallas_call | solution.py:256
Async XLA Ops:
  7.2 67.4 %all-gather.2.cloned.1.call-start = ((), (), s32[]{:S(2)}) async-start(), calls=%async_computation.4 | async-start | bytes 2359296 | tf_op jit(solution)/shard_map/all_gather | solution.py:228
  13.5 118.8 %reduce-scatter.2.cloned.1.call-start = ((), (), s32[]{:S(2)}) async-start(), calls=%async_computation.3 | async-start | bytes 2359296 | tf_op jit(solution)/shard_map/reduce_scatter | solution.py:253
  79.2 5.0 %copy-start = (bf16[2,256,256]{2,1,0:T(8,128)(2,1)S(1)}, bf16[2,256,256]{2,1,0:T(8,128)(2,1)}, u32[]{:S(2)}) copy-start(bf16[2,256,256]{2,1,0:T(8,128)(2,1)} %get-tuple-element.4.masked) | copy-start | bytes 786436
  79.2 53.0 %all-to-all-start.1 = ((bf16[32,256,256]{2,1,0:T(8,128)(2,1)}), bf16[32,256,256]{2,1,0:T(8,128)(2,1)}, u32[]{:S(2)}, u32[]{:S(2)}) async-start(bf16[32,256,256]{2,1,0:T(8,128)(2,1)} %named_pairs.1), calls=%async_computation.2 | async-start | bytes 8388608 | tf_op jit(solution)/shard_map/all_to_all | solution.py:203
  84.2 7.7 %collective-permute-start = (bf16[2,256,256]{2,1,0:T(8,128)(2,1)S(1)}, bf16[2,256,256]{2,1,0:T(8,128)(2,1)S(1)}, u32[]{:S(2)}, u32[]{:S(2)}) collective-permute-start(bf16[2,256,256]{2,1,0:T(8,128)(2,1)S(1)} %copy-done), channel_id=1, source_target_pairs={{0,32},{32,64},{64,96},{96,128},{128,160},{160,192},{192,224},{224... | collective-permute-start | bytes 786440 | tf_op jit(solution)/shard_map/ppermute | solution.py:226
  86.1 7.5 %collective-permute-start.1 = (bf16[2,256,256]{2,1,0:T(8,128)(2,1)S(1)}, bf16[2,256,256]{2,1,0:T(8,128)(2,1)S(1)}, u32[]{:S(2)}, u32[]{:S(2)}) collective-permute-start(bf16[2,256,256]{2,1,0:T(8,128)(2,1)S(1)} %copy-done), channel_id=1, source_target_pairs={{32,0},{64,32},{96,64},{128,96},{160,128},{192,160},{224,192},{256... | collective-permute-start | bytes 786440 | tf_op jit(solution)/shard_map/ppermute | solution.py:227
  91.9 40.4 %copy-start.1 = (bf16[2,256,256]{2,1,0:T(8,128)(2,1)}, bf16[2,256,256]{2,1,0:T(8,128)(2,1)S(1)}, u32[]{:S(2)}) copy-start(bf16[2,256,256]{2,1,0:T(8,128)(2,1)S(1)} %collective-permute-done.lower) | copy-start | bytes 786436
  93.7 38.6 %copy-start.2 = (bf16[2,256,256]{2,1,0:T(8,128)(2,1)}, bf16[2,256,256]{2,1,0:T(8,128)(2,1)S(1)}, u32[]{:S(2)}) copy-start(bf16[2,256,256]{2,1,0:T(8,128)(2,1)S(1)} %collective-permute-done.1.upper) | copy-start | bytes 786436
Sparse Core Ops, SparseCore 0:
  13.6 47.2 all-gather.1
  74.7 45.9 reduce-scatter.1

commit v2 on v1

v2 whole, which is shorter than its diff:
```python
import functools

import jax
import jax.numpy as jnp
from jax import lax
from jax.experimental import pallas as pl
from jax.experimental.pallas import tpu as pltpu
from jax.sharding import PartitionSpec as P

R = 256
NBR = 8
COLS = 4
ROWS = 8
BF = jnp.bfloat16
F32 = jnp.float32
LIMIT = 56 << 20

SMEM = pl.BlockSpec(memory_space=pltpu.SMEM)
VMEM = pl.BlockSpec(memory_space=pltpu.VMEM)
ANY = pl.BlockSpec(memory_space=pl.ANY)


def place():
    dev = lax.axis_index("dev")
    return dev, dev // COLS, dev % COLS


def slot_of(holder):
    return (holder & (COLS - 1)) * ROWS + holder // COLS


def keep_square(rank):
    rows = lax.broadcasted_iota(jnp.int32, (R, R), 0)
    cols = lax.broadcasted_iota(jnp.int32, (R, R), 1)
    return jnp.maximum(rows, cols) < rank


def return_kernel(bucket, nbr, coupling, amps, inter, masked, out, terms, sems):
    dev, _, _ = place()
    pair = pl.program_id(0)

    def copy(pair_at, entry):
        slot = slot_of(nbr[entry, 2 * dev + pair_at] >> 1)
        index = pair_at * NBR + entry
        return pltpu.make_async_copy(terms.at[index], out.at[slot], sems.at[index])

    rank = jnp.left_shift(32, bucket[2 * dev + pair])
    own = jnp.where(keep_square(rank), amps[0].astype(F32), 0.0).astype(BF)
    masked[0] = own
    for entry in range(NBR):
        s = inter[0, entry]
        half = lax.dot_general(s, own, (((0,), (0,)), ((), ())), preferred_element_type=F32)
        term = jnp.dot(half.astype(BF), s, preferred_element_type=F32)
        terms[pair * NBR + entry] = (coupling[pair, entry] * term).astype(BF)
    for entry in range(NBR):
        copy(pair, entry).start()

    @pl.when(pair == 1)
    def _():
        for pair_at in range(2):
            for entry in range(NBR):
                copy(pair_at, entry).wait()


def served_kernel(nbr, served):
    _, y, x = place()
    for i in range(COLS * ROWS):
        served[i] = 0

    def note(i, _):
        giver_x, entry = i // (2 * NBR), i % (2 * NBR)
        name = nbr[entry % NBR, 2 * (y * COLS + giver_x) + entry // NBR]
        holder = name >> 1

        @pl.when((holder & (COLS - 1)) == x)
        def _():
            served[giver_x * ROWS + holder // COLS] = 1 + (name & 1)

        return 0

    lax.fori_loop(0, COLS * 2 * NBR, note, 0)


PIECES = (0, 1, -1, 2, -2, 3, -3, 4)


def select_kernel(served, *rest):
    pieces, out = rest[:ROWS], rest[ROWS]
    column, in_sems, out_sems = rest[ROWS + 1 :]
    _, y, _ = place()
    loads = []
    for at, distance in enumerate(PIECES):
        row = (y + distance) & (ROWS - 1)
        loads.append(
            pltpu.make_async_copy(
                pieces[at], column.at[pl.ds(2 * row, 2)], in_sems.at[at]
            )
        )
    for load in loads:
        load.start()
    for load in loads:
        load.wait()

    def each(act):
        def body(i, _):
            who = served[i]

            @pl.when(who > 0)
            def _():
                pair = 2 * (i & (ROWS - 1)) + who - 1
                act(pltpu.make_async_copy(column.at[pair], out.at[i], out_sems.at[i]))

            return 0

        lax.fori_loop(0, COLS * ROWS, body, 0)

    each(lambda copy: copy.start())
    each(lambda copy: copy.wait())


def combine_kernel(distances, served, arrived, *outs):
    _, y, _ = place()
    for out, group in zip(outs, distances):
        for at, distance in enumerate(group):
            row = (y + distance) & (ROWS - 1)
            totals = [jnp.zeros(out.shape[1:], F32) for _ in range(2)]
            for giver_x in range(COLS):
                value = arrived[giver_x * ROWS + row].astype(F32)
                who = served[giver_x * ROWS + row]
                for side in range(2):
                    totals[side] += jnp.where(who == 1 + side, value, 0.0)
            for side in range(2):
                out[2 * at + side] = totals[side].astype(BF)


def fold_kernel(got_up, got_down, own_up, own_down, send_up, send_down):
    send_up[...] = (own_up[...].astype(F32) + got_up[...].astype(F32)).astype(BF)
    send_down[...] = (own_down[...].astype(F32) + got_down[...].astype(F32)).astype(BF)


def final_kernel(
    bucket,
    nbr,
    coupling,
    edge_local,
    edge_coupling,
    gap,
    masked,
    integrals,
    virt,
    inter,
    edge_inter,
    lower,
    upper,
    terms0,
    terms1,
    terms2,
    terms3,
    terms4,
    terms5,
    named,
    residual,
    new_amps,
    partners,
    sems,
):
    dev, _, _ = place()
    copies = []
    for index in range(2 * NBR):
        slot = slot_of(nbr[index % NBR, 2 * dev + index // NBR] >> 1)
        copies.append(
            pltpu.make_async_copy(named.at[slot], partners.at[index], sems.at[index])
        )
    for copy in copies:
        copy.start()
    for copy in copies:
        copy.wait()

    def project(s, a):
        half = jnp.dot(s, a, preferred_element_type=F32).astype(BF)
        return lax.dot_general(half, s, (((1,), (1,)), ((), ())), preferred_element_type=F32)

    for pair in range(2):
        total = edge_coupling[pair, 0] * project(
            edge_inter[pair, 0], lower[edge_local[pair, 0]]
        )
        total += edge_coupling[pair, 1] * project(
            edge_inter[pair, 1], upper[edge_local[pair, 1]]
        )
        for entry in range(NBR):
            index = pair * NBR + entry
            total += coupling[pair, entry] * project(inter[pair, entry], partners[index])
        energy = jnp.broadcast_to(virt[pair : pair + 1, :], (R, R))
        denom = energy + energy.T + gap[pair]
        own = masked[pair].astype(F32)
        rank = jnp.left_shift(32, bucket[2 * dev + pair])
        keep = keep_square(rank)
        for ref in (terms0, terms1, terms2, terms3, terms4, terms5):
            total += ref[pair].astype(F32)
        value = integrals[pair].astype(F32) + denom * own - total
        value = jnp.where(keep, value, 0.0)
        residual[pair] = value
        new_amps[pair] = jnp.where(keep, own - value / denom, 0.0).astype(BF)


def local(
    amplitudes,
    integrals,
    virt_energy,
    pair_gap,
    rank_bucket,
    neighbours,
    intersection,
    coupling,
    edge_local,
    edge_intersection,
    edge_coupling,
):
    groups = lax.axis_size("grp")
    devices = lax.axis_size("dev")
    nbr = neighbours.T
    rows = [[y * COLS + x for x in range(COLS)] for y in range(ROWS)]

    def swap_columns(value):
        return lax.all_to_all(value, "dev", 0, 0, tiled=True, axis_index_groups=rows)

    def along_y(value, o):
        perm = [(i, (i + o * COLS) % devices) for i in range(devices)]
        return lax.ppermute(value, "dev", perm)

    block = jax.ShapeDtypeStruct((COLS * ROWS, R, R), BF)
    masked, outgoing = pl.pallas_call(
        return_kernel,
        grid=(2,),
        in_specs=[
            SMEM,
            SMEM,
            SMEM,
            pl.BlockSpec((1, R, R), lambda i: (i, 0, 0)),
            pl.BlockSpec((1, NBR, R, R), lambda i: (i, 0, 0, 0)),
        ],
        out_specs=[pl.BlockSpec((1, R, R), lambda i: (i, 0, 0)), ANY],
        out_shape=[jax.ShapeDtypeStruct((2, R, R), BF), block],
        scratch_shapes=[
            pltpu.VMEM((2 * NBR, R, R), BF),
            pltpu.SemaphoreType.DMA((2 * NBR,)),
        ],
        compiler_params=pltpu.CompilerParams(vmem_limit_bytes=LIMIT),
        name="returned_terms",
    )(rank_bucket, nbr, coupling, amplitudes, intersection)
    arrived = swap_columns(outgoing)
    lower = lax.ppermute(masked, "grp", [(i, i + 1) for i in range(groups - 1)])
    upper = lax.ppermute(masked, "grp", [(i + 1, i) for i in range(groups - 1)])
    params = pltpu.CompilerParams(vmem_limit_bytes=LIMIT)
    above2, below2 = along_y(masked, -2), along_y(masked, 2)
    above1, below1, across = along_y(masked, -1), along_y(masked, 1), along_y(masked, 4)
    served = pl.pallas_call(
        served_kernel,
        in_specs=[SMEM],
        out_specs=SMEM,
        out_shape=jax.ShapeDtypeStruct((COLS * ROWS,), jnp.int32),
        name="served_pairs",
    )(nbr)
    above3, below3 = along_y(above2, -1), along_y(below2, 1)
    pieces = (masked, above1, below1, above2, below2, above3, below3, across)
    chosen = pl.pallas_call(
        select_kernel,
        in_specs=[SMEM] + [ANY] * ROWS,
        out_specs=ANY,
        out_shape=block,
        scratch_shapes=[
            pltpu.VMEM((2 * ROWS, R, R), BF),
            pltpu.SemaphoreType.DMA((ROWS,)),
            pltpu.SemaphoreType.DMA((COLS * ROWS,)),
        ],
        compiler_params=params,
        name="named_pairs",
    )(served, *pieces)
    named = swap_columns(chosen)

    def strip(count):
        return pl.BlockSpec((count, R // 4, R), lambda i: (0, i, 0))

    def pairs(count):
        return jax.ShapeDtypeStruct((count, R, R), BF)

    def column_terms(*distances):
        return pl.pallas_call(
            functools.partial(combine_kernel, distances),
            grid=(4,),
            in_specs=[SMEM, strip(COLS * ROWS)],
            out_specs=[strip(2 * len(group)) for group in distances],
            out_shape=[pairs(2 * len(group)) for group in distances],
            compiler_params=params,
            name="column_terms",
        )(served, arrived)

    up, down, across_terms = column_terms((1, 3), (-1, -3), (4,))
    got_up, got_down = along_y(up, 1), along_y(down, -1)
    got_across = along_y(across_terms, 4)
    own, own_up, own_down = column_terms((0,), (2,), (-2,))
    first = pl.BlockSpec((2, R, R), lambda i: (0, 0, 0))
    second = pl.BlockSpec((2, R, R), lambda i: (1, 0, 0))
    send_up, send_down = pl.pallas_call(
        fold_kernel,
        grid=(1,),
        in_specs=[second, second, first, first],
        out_specs=[first, first],
        out_shape=[pairs(2)] * 2,
        compiler_params=params,
        name="folded_terms",
    )(got_up, got_down, own_up, own_down)
    terms = [own, got_up, got_down, got_across, along_y(send_up, 2), along_y(send_down, -2)]
    outputs = pl.pallas_call(
        final_kernel,
        grid=(1,),
        in_specs=[SMEM] * 6 + [VMEM] * 7 + [first] * 6 + [ANY],
        out_specs=[VMEM, VMEM],
        out_shape=[
            jax.ShapeDtypeStruct((2, R, R), F32),
            jax.ShapeDtypeStruct((2, R, R), BF),
        ],
        scratch_shapes=[
            pltpu.VMEM((2 * NBR, R, R), BF),
            pltpu.SemaphoreType.DMA((2 * NBR,)),
        ],
        compiler_params=pltpu.CompilerParams(vmem_limit_bytes=LIMIT),
        name="residual_update",
    )(
        rank_bucket,
        nbr,
        coupling,
        edge_local,
        edge_coupling,
        pair_gap,
        masked,
        integrals,
        virt_energy,
        intersection,
        edge_intersection,
        lower,
        upper,
        *terms,
        named,
    )
    return tuple(outputs)


def solution(mesh):
    pair = P(("grp", "dev"))
    placed = (pair, pair, pair, pair, P("grp"), P("grp")) + (pair,) * 5
    return jax.shard_map(
        local, mesh=mesh, in_specs=placed, out_specs=(pair, pair), check_vma=False
    )
```

time: 149 us -> 132 us (0.89)
  the two profiles are of different devices: /device:TPU:72 before, /device:TPU:464 now
where the time goes in v2:
time: 132 us; the launch traced here: 131 us
  starting transfers between devices  66 us (50%)
  waiting for transfers between devices  32 us (24%)
  Pallas kernels  29.8 us (23%)
  local copies, waits for them, and re-layouts  2.21 us (2%)
    ppermute x12, starting transfers between devices, along_y(): return lax.ppermute(value, 'dev', perm)  51.7 us
    ppermute x12, waiting for transfers between devices, along_y(): return lax.ppermute(value, 'dev', perm)  30.2 us
    all_to_all x2, starting transfers between devices, swap_columns(): lax.all_to_all(value, 'dev', 0, 0, tiled=True, axis_index_groups=rows)  9.92 us
    pallas_call x2, Pallas kernels, column_terms(): pl.pallas_call(functools.partial(combine_kernel, distances), grid=(4,), i...  8.77 us
    pallas_call x1, Pallas kernels, local(): pl.pallas_call(final_kernel, grid=(1,), in_specs=[SMEM] * 6 + [VMEM] * 7...  7.07 us
    pallas_call x1, Pallas kernels, local(): pl.pallas_call(return_kernel, grid=(2,), in_specs=[SMEM, SMEM, SMEM, pl.B...  4.84 us
    pallas_call x1, Pallas kernels, local(): pl.pallas_call(select_kernel, in_specs=[SMEM] + [ANY] * ROWS, out_specs=A...  4.09 us
    pallas_call x1, Pallas kernels, local(): pl.pallas_call(served_kernel, in_specs=[SMEM], out_specs=SMEM, out_shape=...  2.95 us
  transfers between devices with their start and end apart: 16, of which 7 were waited for; matrix products, arithmetic and copies ran while one was open for 0% of the time, Pallas kernels for 14%

profile of v2, /device:TPU:464, one launch (start us, length us, event | category | flops | bytes accessed | tf_op | source)
XLA Modules:
  0.0 131.0 jit_solution(18038782564038125158)
XLA Ops:
  0.6 4.8 %returned_terms.1 = (bf16[2,256,256]{2,1,0:T(8,128)(2,1)}, bf16[32,256,256]{2,1,0:T(8,128)(2,1)}) custom-call(s32[64]{0:T(128)} %bucket.3, s32[8,64]{1,0:T(8,128)} %bitcast.1, f32[2,8]{1,0:T(2,128)} %coupling.3, bf16[2,256,256]{2,1,0:T(8,128)(2,1)} %amps.1, bf16[2,8,256,256]{3,2,1,0:T(8,128)(2,1)} %inter.3), custom_call_target="tpu_custom_call" | custom-call | tf_op jit(solution)/shard_map/returned_terms/pallas_call | solution.py:232
  5.5 5.0 %all-to-all-start = ((bf16[32,256,256]{2,1,0:T(8,128)(2,1)}), bf16[32,256,256]{2,1,0:T(8,128)(2,1)}, u32[]{:S(2)}, u32[]{:S(2)}) async-start(bf16[32,256,256]{2,1,0:T(8,128)(2,1)} %get-tuple-element.13), calls=%async_computation | async-start | bytes 8388608 | tf_op jit(solution)/shard_map/all_to_all | solution.py:225
  10.5 5.7 %collective-permute-start.10 = (bf16[2,256,256]{2,1,0:T(8,128)(2,1)S(1)}, bf16[2,256,256]{2,1,0:T(8,128)(2,1)S(1)}, u32[]{:S(2)}, u32[]{:S(2)}) collective-permute-start(bf16[2,256,256]{2,1,0:T(8,128)(2,1)S(1)} %copy-done.2), channel_id=1, source_target_pairs={{0,8},{1,9},{2,10},{3,11},{4,12},{5,13},{6,14},{7,15},{8,16},{9,17... | collective-permute-start | bytes 786440 | tf_op jit(solution)/shard_map/ppermute | solution.py:229
  18.2 5.1 %collective-permute-start.13 = (bf16[2,256,256]{2,1,0:T(8,128)(2,1)S(1)}, bf16[2,256,256]{2,1,0:T(8,128)(2,1)S(1)}, u32[]{:S(2)}, u32[]{:S(2)}) collective-permute-start(bf16[2,256,256]{2,1,0:T(8,128)(2,1)S(1)} %copy-done.2), channel_id=1, source_target_pairs={{0,16},{1,17},{2,18},{3,19},{4,20},{5,21},{6,22},{7,23},{8,24},{9,... | collective-permute-start | bytes 786440 | tf_op jit(solution)/shard_map/ppermute | solution.py:229
  23.3 2.6 %collective-permute-start.8 = (bf16[2,256,256]{2,1,0:T(8,128)(2,1)S(1)}, bf16[2,256,256]{2,1,0:T(8,128)(2,1)S(1)}, u32[]{:S(2)}, u32[]{:S(2)}) collective-permute-start(bf16[2,256,256]{2,1,0:T(8,128)(2,1)S(1)} %copy-done.2), channel_id=1, source_target_pairs={{0,4},{1,5},{2,6},{3,7},{4,8},{5,9},{6,10},{7,11},{8,12},{9,13},{1... | collective-permute-start | bytes 786440 | tf_op jit(solution)/shard_map/ppermute | solution.py:229
  25.9 3.8 %collective-permute-start.7 = (bf16[2,256,256]{2,1,0:T(8,128)(2,1)S(1)}, bf16[2,256,256]{2,1,0:T(8,128)(2,1)S(1)}, u32[]{:S(2)}, u32[]{:S(2)}) collective-permute-start(bf16[2,256,256]{2,1,0:T(8,128)(2,1)S(1)} %copy-done.2), channel_id=1, source_target_pairs={{0,28},{1,29},{2,30},{3,31},{4,0},{5,1},{6,2},{7,3},{8,4},{9,5},{1... | collective-permute-start | bytes 786440 | tf_op jit(solution)/shard_map/ppermute | solution.py:229
  29.7 2.1 %collective-permute-start.12 = (bf16[2,256,256]{2,1,0:T(8,128)(2,1)S(1)}, bf16[2,256,256]{2,1,0:T(8,128)(2,1)S(1)}, u32[]{:S(2)}, u32[]{:S(2)}) collective-permute-start(bf16[2,256,256]{2,1,0:T(8,128)(2,1)S(1)} %collective-permute-done.10.rest_4_), channel_id=1, source_target_pairs={{0,4},{1,5},{2,6},{3,7},{4,8},{5,9},{6,10},{7,11},{8,12},{9,13},{1... | collective-permute-start | bytes 786440 | tf_op jit(solution)/shard_map/ppermute | solution.py:229
  31.8 14.0 %collective-permute-done.9.rest_3_ = bf16[2,256,256]{2,1,0:T(8,128)(2,1)S(1)} collective-permute-done((bf16[2,256,256]{2,1,0:T(8,128)(2,1)S(1)}, bf16[2,256,256]{2,1,0:T(8,128)(2,1)S(1)}, u32[]{:S(2)}, u32[]{:S(2)}) %collective-permute-start.9) | collective-permute-done | bytes 262176 | tf_op jit(solution)/shard_map/ppermute | solution.py:229
  47.7 2.9 %served_pairs.1.served = s32[32]{0:T(128)} custom-call(s32[8,64]{1,0:T(8,128)} %bitcast.2), custom_call_target="tpu_custom_call" | custom-call | tf_op jit(solution)/shard_map/served_pairs/pallas_call | solution.py:257
  50.8 3.3 %collective-permute-done.11.rest_5_ = bf16[2,256,256]{2,1,0:T(8,128)(2,1)S(1)} collective-permute-done((bf16[2,256,256]{2,1,0:T(8,128)(2,1)S(1)}, bf16[2,256,256]{2,1,0:T(8,128)(2,1)S(1)}, u32[]{:S(2)}, u32[]{:S(2)}) %collective-permute-start.11) | collective-permute-done | bytes 262176 | tf_op jit(solution)/shard_map/ppermute | solution.py:229
  54.8 4.1 %named_pairs.1 = bf16[32,256,256]{2,1,0:T(8,128)(2,1)} custom-call(s32[32]{0:T(128)} %served_pairs.1.served, bf16[2,256,256]{2,1,0:T(8,128)(2,1)} %get-tuple-element.12.rest_0_.masked, bf16[2,256,256]{2,1,0:T(8,128)(2,1)} %copy-done.13, bf16[2,256,256]{2,1,0:T(8,128)(2,1)} %copy-done.11, bf16[2,256,256]{2,1,0:T(8,128)(2,1)} %copy-done.8, ...), custom_call_target="tpu_custom_call" | custom-call | tf_op jit(solution)/shard_map/named_pairs/pallas_call | solution.py:266
  59.7 4.9 %all-to-all-start.1 = ((bf16[32,256,256]{2,1,0:T(8,128)(2,1)}), bf16[32,256,256]{2,1,0:T(8,128)(2,1)}, u32[]{:S(2)}, u32[]{:S(2)}) async-start(bf16[32,256,256]{2,1,0:T(8,128)(2,1)} %named_pairs.1), calls=%async_computation.1 | async-start | bytes 8388608 | tf_op jit(solution)/shard_map/all_to_all | solution.py:225
  64.6 4.5 %column_terms.3 = (bf16[4,256,256]{2,1,0:T(8,128)(2,1)}, bf16[4,256,256]{2,1,0:T(8,128)(2,1)}, bf16[2,256,256]{2,1,0:T(8,128)(2,1)}) custom-call(s32[32]{0:T(128)} %served_pairs.1.served, bf16[32,256,256]{2,1,0:T(8,128)(2,1)} %all-to-all-done.arrived), custom_call_target="tpu_custom_call" | custom-call | tf_op jit(solution)/shard_map/column_terms/pallas_call | solution.py:288
  69.1 3.7 %collective-permute-start.2 = (bf16[4,256,256]{2,1,0:T(8,128)(2,1)}, bf16[4,256,256]{2,1,0:T(8,128)(2,1)S(1)}, u32[]{:S(2)}, u32[]{:S(2)}) collective-permute-start(bf16[4,256,256]{2,1,0:T(8,128)(2,1)} %get-tuple-element.15), channel_id=1, source_target_pairs={{0,4},{1,5},{2,6},{3,7},{4,8},{5,9},{6,10},{7,11},{8,12},{9,13},{1... | collective-permute-start | bytes 1572872 | tf_op jit(solution)/shard_map/ppermute | solution.py:229
  72.9 2.1 %collective-permute-start.3 = (bf16[4,256,256]{2,1,0:T(8,128)(2,1)}, bf16[4,256,256]{2,1,0:T(8,128)(2,1)S(1)}, u32[]{:S(2)}, u32[]{:S(2)}) collective-permute-start(bf16[4,256,256]{2,1,0:T(8,128)(2,1)} %get-tuple-element.16), channel_id=1, source_target_pairs={{0,28},{1,29},{2,30},{3,31},{4,0},{5,1},{6,2},{7,3},{8,4},{9,5},{1... | collective-permute-start | bytes 1572872 | tf_op jit(solution)/shard_map/ppermute | solution.py:229
  76.9 2.4 %collective-permute-start = (bf16[2,256,256]{2,1,0:T(8,128)(2,1)S(1)}, bf16[2,256,256]{2,1,0:T(8,128)(2,1)S(1)}, u32[]{:S(2)}, u32[]{:S(2)}) collective-permute-start(bf16[2,256,256]{2,1,0:T(8,128)(2,1)S(1)} %copy-done.3), channel_id=1, source_target_pairs={{0,32},{32,64},{64,96},{96,128},{128,160},{160,192},{192,224},{224... | collective-permute-start | bytes 786440 | tf_op jit(solution)/shard_map/ppermute | solution.py:252
  79.4 5.9 %collective-permute-start.4 = (bf16[2,256,256]{2,1,0:T(8,128)(2,1)}, bf16[2,256,256]{2,1,0:T(8,128)(2,1)S(1)}, u32[]{:S(2)}, u32[]{:S(2)}) collective-permute-start(bf16[2,256,256]{2,1,0:T(8,128)(2,1)} %get-tuple-element.17), channel_id=1, source_target_pairs={{0,16},{1,17},{2,18},{3,19},{4,20},{5,21},{6,22},{7,23},{8,24},{9,... | collective-permute-start | bytes 786440 | tf_op jit(solution)/shard_map/ppermute | solution.py:229
  85.3 4.2 %column_terms.2 = (bf16[2,256,256]{2,1,0:T(8,128)(2,1)}, bf16[2,256,256]{2,1,0:T(8,128)(2,1)}, bf16[2,256,256]{2,1,0:T(8,128)(2,1)}) custom-call(s32[32]{0:T(128)} %served_pairs.1.served, bf16[32,256,256]{2,1,0:T(8,128)(2,1)} %all-to-all-done.arrived), custom_call_target="tpu_custom_call" | custom-call | tf_op jit(solution)/shard_map/column_terms/pallas_call | solution.py:288
  89.5 2.5 %collective-permute-done.3.got_down.terms2 = bf16[4,256,256]{2,1,0:T(8,128)(2,1)S(1)} collective-permute-done((bf16[4,256,256]{2,1,0:T(8,128)(2,1)}, bf16[4,256,256]{2,1,0:T(8,128)(2,1)S(1)}, u32[]{:S(2)}, u32[]{:S(2)}) %collective-permute-start.3) | collective-permute-done | bytes 524320 | tf_op jit(solution)/shard_map/ppermute | solution.py:229
  92.8 2.0 %folded_terms.1 = (bf16[2,256,256]{2,1,0:T(8,128)(2,1)}, bf16[2,256,256]{2,1,0:T(8,128)(2,1)}) custom-call(bf16[4,256,256]{2,1,0:T(8,128)(2,1)} %copy-done, bf16[4,256,256]{2,1,0:T(8,128)(2,1)} %copy-done.1, bf16[2,256,256]{2,1,0:T(8,128)(2,1)} %get-tuple-element.18.own_up, bf16[2,256,256]{2,1,0:T(8,128)(2,1)} %get-tuple-element.19.own_down), custom_call_target="tpu_custom_call" | custom-call | tf_op jit(solution)/shard_map/folded_terms/pallas_call | solution.py:304
  94.8 15.0 %collective-permute-start.5 = (bf16[2,256,256]{2,1,0:T(8,128)(2,1)}, bf16[2,256,256]{2,1,0:T(8,128)(2,1)S(1)}, u32[]{:S(2)}, u32[]{:S(2)}) collective-permute-start(bf16[2,256,256]{2,1,0:T(8,128)(2,1)} %get-tuple-element.20), channel_id=1, source_target_pairs={{0,8},{1,9},{2,10},{3,11},{4,12},{5,13},{6,14},{7,15},{8,16},{9,17... | collective-permute-start | bytes 786440 | tf_op jit(solution)/shard_map/ppermute | solution.py:229
  112.9 4.0 %collective-permute-done.5.terms4 = bf16[2,256,256]{2,1,0:T(8,128)(2,1)S(1)} collective-permute-done((bf16[2,256,256]{2,1,0:T(8,128)(2,1)}, bf16[2,256,256]{2,1,0:T(8,128)(2,1)S(1)}, u32[]{:S(2)}, u32[]{:S(2)}) %collective-permute-start.5) | collective-permute-done | bytes 262176 | tf_op jit(solution)/shard_map/ppermute | solution.py:229
  116.9 6.4 %collective-permute-done.6.terms5 = bf16[2,256,256]{2,1,0:T(8,128)(2,1)S(1)} collective-permute-done((bf16[2,256,256]{2,1,0:T(8,128)(2,1)}, bf16[2,256,256]{2,1,0:T(8,128)(2,1)S(1)}, u32[]{:S(2)}, u32[]{:S(2)}) %collective-permute-start.6) | collective-permute-done | bytes 262176 | tf_op jit(solution)/shard_map/ppermute | solution.py:229
  123.9 7.1 %residual_update.1 = (f32[2,256,256]{2,1,0:T(8,128)}, bf16[2,256,256]{2,1,0:T(8,128)(2,1)}) custom-call(s32[64]{0:T(128)} %bucket.3, s32[8,64]{1,0:T(8,128)} %bitcast.3, f32[2,8]{1,0:T(2,128)} %coupling.3, s32[2,2]{1,0:T(2,128)} %edge_local.1, f32[2,2]{1,0:T(2,128)} %edge_coupling.1, f32[2]{0:T(128)} %gap.1, ...), custom_call_target="tpu_custom_call" | custom-call | tf_op jit(solution)/shard_map/residual_update/pallas_call | solution.py:314
  (47 shorter events, 11.8 us)
Async XLA Ops:
  5.5 5.0 %copy-start.2 = (bf16[2,256,256]{2,1,0:T(8,128)(2,1)S(1)}, bf16[2,256,256]{2,1,0:T(8,128)(2,1)}, u32[]{:S(2)}) copy-start(bf16[2,256,256]{2,1,0:T(8,128)(2,1)} %get-tuple-element.12.rest_0_.masked) | copy-start | bytes 786436
  5.5 54.2 %all-to-all-start = ((bf16[32,256,256]{2,1,0:T(8,128)(2,1)}), bf16[32,256,256]{2,1,0:T(8,128)(2,1)}, u32[]{:S(2)}, u32[]{:S(2)}) async-start(bf16[32,256,256]{2,1,0:T(8,128)(2,1)} %get-tuple-element.13), calls=%async_computation | async-start | bytes 8388608 | tf_op jit(solution)/shard_map/all_to_all | solution.py:225
  10.5 19.1 %collective-permute-start.10 = (bf16[2,256,256]{2,1,0:T(8,128)(2,1)S(1)}, bf16[2,256,256]{2,1,0:T(8,128)(2,1)S(1)}, u32[]{:S(2)}, u32[]{:S(2)}) collective-permute-start(bf16[2,256,256]{2,1,0:T(8,128)(2,1)S(1)} %copy-done.2), channel_id=1, source_target_pairs={{0,8},{1,9},{2,10},{3,11},{4,12},{5,13},{6,14},{7,15},{8,16},{9,17... | collective-permute-start | bytes 786440 | tf_op jit(solution)/shard_map/ppermute | solution.py:229
  16.3 29.6 %collective-permute-start.9 = (bf16[2,256,256]{2,1,0:T(8,128)(2,1)S(1)}, bf16[2,256,256]{2,1,0:T(8,128)(2,1)S(1)}, u32[]{:S(2)}, u32[]{:S(2)}) collective-permute-start(bf16[2,256,256]{2,1,0:T(8,128)(2,1)S(1)} %copy-done.2), channel_id=1, source_target_pairs={{0,24},{1,25},{2,26},{3,27},{4,28},{5,29},{6,30},{7,31},{8,0},{9,1... | collective-permute-start | bytes 786440 | tf_op jit(solution)/shard_map/ppermute | solution.py:229
  18.2 32.5 %collective-permute-start.13 = (bf16[2,256,256]{2,1,0:T(8,128)(2,1)S(1)}, bf16[2,256,256]{2,1,0:T(8,128)(2,1)S(1)}, u32[]{:S(2)}, u32[]{:S(2)}) collective-permute-start(bf16[2,256,256]{2,1,0:T(8,128)(2,1)S(1)} %copy-done.2), channel_id=1, source_target_pairs={{0,16},{1,17},{2,18},{3,19},{4,20},{5,21},{6,22},{7,23},{8,24},{9,... | collective-permute-start | bytes 786440 | tf_op jit(solution)/shard_map/ppermute | solution.py:229
  23.3 27.5 %collective-permute-start.8 = (bf16[2,256,256]{2,1,0:T(8,128)(2,1)S(1)}, bf16[2,256,256]{2,1,0:T(8,128)(2,1)S(1)}, u32[]{:S(2)}, u32[]{:S(2)}) collective-permute-start(bf16[2,256,256]{2,1,0:T(8,128)(2,1)S(1)} %copy-done.2), channel_id=1, source_target_pairs={{0,4},{1,5},{2,6},{3,7},{4,8},{5,9},{6,10},{7,11},{8,12},{9,13},{1... | collective-permute-start | bytes 786440 | tf_op jit(solution)/shard_map/ppermute | solution.py:229
  25.9 24.8 %collective-permute-start.7 = (bf16[2,256,256]{2,1,0:T(8,128)(2,1)S(1)}, bf16[2,256,256]{2,1,0:T(8,128)(2,1)S(1)}, u32[]{:S(2)}, u32[]{:S(2)}) collective-permute-start(bf16[2,256,256]{2,1,0:T(8,128)(2,1)S(1)} %copy-done.2), channel_id=1, source_target_pairs={{0,28},{1,29},{2,30},{3,31},{4,0},{5,1},{6,2},{7,3},{8,4},{9,5},{1... | collective-permute-start | bytes 786440 | tf_op jit(solution)/shard_map/ppermute | solution.py:229
  29.7 24.4 %copy-start.7 = (bf16[2,256,256]{2,1,0:T(8,128)(2,1)}, bf16[2,256,256]{2,1,0:T(8,128)(2,1)S(1)}, u32[]{:S(2)}) copy-start(bf16[2,256,256]{2,1,0:T(8,128)(2,1)S(1)} %collective-permute-done.10.rest_4_) | copy-start | bytes 786436
  29.7 21.1 %collective-permute-start.12 = (bf16[2,256,256]{2,1,0:T(8,128)(2,1)S(1)}, bf16[2,256,256]{2,1,0:T(8,128)(2,1)S(1)}, u32[]{:S(2)}, u32[]{:S(2)}) collective-permute-start(bf16[2,256,256]{2,1,0:T(8,128)(2,1)S(1)} %collective-permute-done.10.rest_4_), channel_id=1, source_target_pairs={{0,4},{1,5},{2,6},{3,7},{4,8},{5,9},{6,10},{7,11},{8,12},{9,13},{1... | collective-permute-start | bytes 786440 | tf_op jit(solution)/shard_map/ppermute | solution.py:229
  45.8 8.3 %copy-start.8 = (bf16[2,256,256]{2,1,0:T(8,128)(2,1)}, bf16[2,256,256]{2,1,0:T(8,128)(2,1)S(1)}, u32[]{:S(2)}) copy-start(bf16[2,256,256]{2,1,0:T(8,128)(2,1)S(1)} %collective-permute-done.9.rest_3_) | copy-start | bytes 786436
  45.8 8.3 %collective-permute-start.11 = (bf16[2,256,256]{2,1,0:T(8,128)(2,1)S(1)}, bf16[2,256,256]{2,1,0:T(8,128)(2,1)S(1)}, u32[]{:S(2)}, u32[]{:S(2)}) collective-permute-start(bf16[2,256,256]{2,1,0:T(8,128)(2,1)S(1)} %collective-permute-done.9.rest_3_), channel_id=1, source_target_pairs={{0,28},{1,29},{2,30},{3,31},{4,0},{5,1},{6,2},{7,3},{8,4},{9,5},{1... | collective-permute-start | bytes 786440 | tf_op jit(solution)/shard_map/ppermute | solution.py:229
  59.7 53.2 %all-to-all-start.1 = ((bf16[32,256,256]{2,1,0:T(8,128)(2,1)}), bf16[32,256,256]{2,1,0:T(8,128)(2,1)}, u32[]{:S(2)}, u32[]{:S(2)}) async-start(bf16[32,256,256]{2,1,0:T(8,128)(2,1)} %named_pairs.1), calls=%async_computation.1 | async-start | bytes 8388608 | tf_op jit(solution)/shard_map/all_to_all | solution.py:225
  64.6 10.4 %copy-start.3 = (bf16[2,256,256]{2,1,0:T(8,128)(2,1)S(1)}, bf16[2,256,256]{2,1,0:T(8,128)(2,1)}, u32[]{:S(2)}) copy-start(bf16[2,256,256]{2,1,0:T(8,128)(2,1)} %get-tuple-element.12.rest_0_.masked) | copy-start | bytes 786436
  69.1 20.4 %collective-permute-start.2 = (bf16[4,256,256]{2,1,0:T(8,128)(2,1)}, bf16[4,256,256]{2,1,0:T(8,128)(2,1)S(1)}, u32[]{:S(2)}, u32[]{:S(2)}) collective-permute-start(bf16[4,256,256]{2,1,0:T(8,128)(2,1)} %get-tuple-element.15), channel_id=1, source_target_pairs={{0,4},{1,5},{2,6},{3,7},{4,8},{5,9},{6,10},{7,11},{8,12},{9,13},{1... | collective-permute-start | bytes 1572872 | tf_op jit(solution)/shard_map/ppermute | solution.py:229
  72.9 19.1 %collective-permute-start.3 = (bf16[4,256,256]{2,1,0:T(8,128)(2,1)}, bf16[4,256,256]{2,1,0:T(8,128)(2,1)S(1)}, u32[]{:S(2)}, u32[]{:S(2)}) collective-permute-start(bf16[4,256,256]{2,1,0:T(8,128)(2,1)} %get-tuple-element.16), channel_id=1, source_target_pairs={{0,28},{1,29},{2,30},{3,31},{4,0},{5,1},{6,2},{7,3},{8,4},{9,5},{1... | collective-permute-start | bytes 1572872 | tf_op jit(solution)/shard_map/ppermute | solution.py:229
  75.0 36.7 %collective-permute-start.1 = (bf16[2,256,256]{2,1,0:T(8,128)(2,1)S(1)}, bf16[2,256,256]{2,1,0:T(8,128)(2,1)S(1)}, u32[]{:S(2)}, u32[]{:S(2)}) collective-permute-start(bf16[2,256,256]{2,1,0:T(8,128)(2,1)S(1)} %copy-done.3), channel_id=1, source_target_pairs={{32,0},{64,32},{96,64},{128,96},{160,128},{192,160},{224,192},{256... | collective-permute-start | bytes 786440 | tf_op jit(solution)/shard_map/ppermute | solution.py:253
  76.9 34.8 %collective-permute-start = (bf16[2,256,256]{2,1,0:T(8,128)(2,1)S(1)}, bf16[2,256,256]{2,1,0:T(8,128)(2,1)S(1)}, u32[]{:S(2)}, u32[]{:S(2)}) collective-permute-start(bf16[2,256,256]{2,1,0:T(8,128)(2,1)S(1)} %copy-done.3), channel_id=1, source_target_pairs={{0,32},{32,64},{64,96},{96,128},{128,160},{160,192},{192,224},{224... | collective-permute-start | bytes 786440 | tf_op jit(solution)/shard_map/ppermute | solution.py:252
  79.4 32.4 %collective-permute-start.4 = (bf16[2,256,256]{2,1,0:T(8,128)(2,1)}, bf16[2,256,256]{2,1,0:T(8,128)(2,1)S(1)}, u32[]{:S(2)}, u32[]{:S(2)}) collective-permute-start(bf16[2,256,256]{2,1,0:T(8,128)(2,1)} %get-tuple-element.17), channel_id=1, source_target_pairs={{0,16},{1,17},{2,18},{3,19},{4,20},{5,21},{6,22},{7,23},{8,24},{9,... | collective-permute-start | bytes 786440 | tf_op jit(solution)/shard_map/ppermute | solution.py:229
  94.8 22.0 %collective-permute-start.5 = (bf16[2,256,256]{2,1,0:T(8,128)(2,1)}, bf16[2,256,256]{2,1,0:T(8,128)(2,1)S(1)}, u32[]{:S(2)}, u32[]{:S(2)}) collective-permute-start(bf16[2,256,256]{2,1,0:T(8,128)(2,1)} %get-tuple-element.20), channel_id=1, source_target_pairs={{0,8},{1,9},{2,10},{3,11},{4,12},{5,13},{6,14},{7,15},{8,16},{9,17... | collective-permute-start | bytes 786440 | tf_op jit(solution)/shard_map/ppermute | solution.py:229
  109.8 13.4 %collective-permute-start.6 = (bf16[2,256,256]{2,1,0:T(8,128)(2,1)}, bf16[2,256,256]{2,1,0:T(8,128)(2,1)S(1)}, u32[]{:S(2)}, u32[]{:S(2)}) collective-permute-start(bf16[2,256,256]{2,1,0:T(8,128)(2,1)} %get-tuple-element.21), channel_id=1, source_target_pairs={{0,24},{1,25},{2,26},{3,27},{4,28},{5,29},{6,30},{7,31},{8,0},{9,1... | collective-permute-start | bytes 786440 | tf_op jit(solution)/shard_map/ppermute | solution.py:229
  111.8 11.5 %copy-start.4 = (bf16[2,256,256]{2,1,0:T(8,128)(2,1)}, bf16[2,256,256]{2,1,0:T(8,128)(2,1)S(1)}, u32[]{:S(2)}) copy-start(bf16[2,256,256]{2,1,0:T(8,128)(2,1)S(1)} %collective-permute-done.1.upper) | copy-start | bytes 786436
  111.8 11.4 %copy-start.5 = (bf16[2,256,256]{2,1,0:T(8,128)(2,1)}, bf16[2,256,256]{2,1,0:T(8,128)(2,1)S(1)}, u32[]{:S(2)}) copy-start(bf16[2,256,256]{2,1,0:T(8,128)(2,1)S(1)} %collective-permute-done.lower) | copy-start | bytes 786436
  111.8 11.4 %copy-start.6 = (bf16[2,256,256]{2,1,0:T(8,128)(2,1)}, bf16[2,256,256]{2,1,0:T(8,128)(2,1)S(1)}, u32[]{:S(2)}) copy-start(bf16[2,256,256]{2,1,0:T(8,128)(2,1)S(1)} %collective-permute-done.4.terms3) | copy-start | bytes 786436
  116.9 6.4 %copy-start.10 = (bf16[2,256,256]{2,1,0:T(8,128)(2,1)}, bf16[2,256,256]{2,1,0:T(8,128)(2,1)S(1)}, u32[]{:S(2)}) copy-start(bf16[2,256,256]{2,1,0:T(8,128)(2,1)S(1)} %collective-permute-done.5.terms4) | copy-start | bytes 786436
  (8 other events, 18.1 us)

commit v3 on v2

v3 whole, which is shorter than its diff:
```python
import functools

import jax
import jax.numpy as jnp
from jax import lax
from jax.experimental import pallas as pl
from jax.experimental.pallas import tpu as pltpu
from jax.sharding import PartitionSpec as P

R = 256
NBR = 8
COLS = 4
ROWS = 8
BF = jnp.bfloat16
F32 = jnp.float32
LIMIT = 56 << 20

SMEM = pl.BlockSpec(memory_space=pltpu.SMEM)
VMEM = pl.BlockSpec(memory_space=pltpu.VMEM)
ANY = pl.BlockSpec(memory_space=pl.ANY)


def place():
    dev = lax.axis_index("dev")
    return dev, dev // COLS, dev % COLS


def slot_of(holder):
    return (holder & (COLS - 1)) * ROWS + holder // COLS


def keep_square(rank):
    rows = lax.broadcasted_iota(jnp.int32, (R, R), 0)
    cols = lax.broadcasted_iota(jnp.int32, (R, R), 1)
    return jnp.maximum(rows, cols) < rank


def times_transposed(a, b):
    return lax.dot_general(a, b, (((1,), (1,)), ((), ())), preferred_element_type=F32)


def return_kernel(bucket, nbr, coupling, amps, inter, masked, out, terms, sems):
    dev, _, _ = place()
    pair = pl.program_id(0)

    def copy(pair_at, entry):
        slot = slot_of(nbr[entry, 2 * dev + pair_at] >> 1)
        index = pair_at * NBR + entry
        return pltpu.make_async_copy(terms.at[index], out.at[slot], sems.at[index])

    rank = jnp.left_shift(32, bucket[2 * dev + pair])
    own = jnp.where(keep_square(rank), amps[0].astype(F32), 0.0).astype(BF)
    masked[0] = own
    for entry in range(NBR):
        s = inter[0, entry]
        half = lax.dot_general(s, own, (((0,), (0,)), ((), ())), preferred_element_type=F32)
        term = jnp.dot(half.astype(BF), s, preferred_element_type=F32)
        terms[pair * NBR + entry] = (coupling[pair, entry] * term).astype(BF)
    for entry in range(NBR):
        copy(pair, entry).start()

    @pl.when(pair == 1)
    def _():
        for pair_at in range(2):
            for entry in range(NBR):
                copy(pair_at, entry).wait()


def served_kernel(nbr, served):
    _, y, x = place()
    spare = COLS * ROWS
    for i in range(spare):
        served[i] = 0
    for giver_x in range(COLS):
        for entry in range(2 * NBR):
            name = nbr[entry % NBR, 2 * (y * COLS + giver_x) + entry // NBR]
            holder = name >> 1
            hit = (holder & (COLS - 1)) == x
            at = jnp.where(hit, giver_x * ROWS + (holder >> 2), spare)
            served[at] = 1 + (name & 1)


PIECES = (0, 1, -1, 2, -2, 3, -3)


def select_kernel(served, *rest):
    pieces, out = rest[: ROWS + 1], rest[ROWS + 1]
    column, in_sems, out_sems = rest[ROWS + 2 :]
    _, y, _ = place()
    loads = []
    for at, distance in enumerate(PIECES):
        row = (y + distance) & (ROWS - 1)
        loads.append(
            pltpu.make_async_copy(
                pieces[at], column.at[pl.ds(2 * row, 2)], in_sems.at[at]
            )
        )
    far = (y + ROWS // 2) & (ROWS - 1)
    for side in range(2):
        at = ROWS - 1 + side
        rows = column.at[pl.ds(2 * far + side, 1)]
        loads.append(pltpu.make_async_copy(pieces[at], rows, in_sems.at[at]))
    for load in loads:
        load.start()
    for load in loads:
        load.wait()

    def each(act):
        def body(i, _):
            who = served[i]

            @pl.when(who > 0)
            def _():
                pair = 2 * (i & (ROWS - 1)) + who - 1
                act(pltpu.make_async_copy(column.at[pair], out.at[i], out_sems.at[i]))

            return 0

        lax.fori_loop(0, COLS * ROWS, body, 0)

    each(lambda copy: copy.start())
    each(lambda copy: copy.wait())


def combine_kernel(distances, served, arrived, *rest):
    outs, (slots, sems) = rest[: len(distances)], rest[len(distances) :]
    _, y, _ = place()
    order = [distance for group in distances for distance, _ in group]

    def fetches(at, act):
        row = (y + order[at]) & (ROWS - 1)
        for giver_x in range(COLS):
            copy = pltpu.make_async_copy(
                arrived.at[giver_x * ROWS + row],
                slots.at[at * COLS + giver_x],
                sems.at[at * COLS + giver_x],
            )
            pl.when(served[giver_x * ROWS + row] > 0)(functools.partial(act, copy))

    for at in range(len(order)):
        fetches(at, lambda copy: copy.start())
    at = 0
    for out, group in zip(outs, distances):
        put = 0
        for distance, sides in group:
            fetches(at, lambda copy: copy.wait())
            row = (y + distance) & (ROWS - 1)
            for chunk in range(0, R, 64):
                part = pl.ds(chunk, 64)
                totals = [jnp.zeros((64, R), F32) for _ in sides]
                for giver_x in range(COLS):
                    value = slots[at * COLS + giver_x, part, :].astype(F32)
                    who = served[giver_x * ROWS + row]
                    for i, side in enumerate(sides):
                        totals[i] += jnp.where(who == 1 + side, value, 0.0)
                for i, total in enumerate(totals):
                    out[put + i, part, :] = total.astype(BF)
            put += len(sides)
            at += 1


def fold_kernel(got_up, got_down, far_up, far_down, own_up, own_down, send_up, send_down):
    for side in range(2):
        ups = own_up[side].astype(F32) + got_up[side].astype(F32)
        downs = own_down[side].astype(F32) + got_down[side].astype(F32)
        if side == 0:
            ups += far_up[0].astype(F32)
        else:
            downs += far_down[0].astype(F32)
        send_up[side] = ups.astype(BF)
        send_down[side] = downs.astype(BF)


def project(s, a):
    half = jnp.dot(s, a, preferred_element_type=F32).astype(BF)
    return times_transposed(half, s)


def gap_matrix(virt, gap, pair):
    energy = jnp.broadcast_to(virt[pl.ds(pair, 1), :], (R, R))
    return energy + energy.T + gap[pair]


def edge_kernel(
    edge_local, edge_coupling, gap, masked, integrals, virt, edge_inter, lower, upper, partial
):
    pair = pl.program_id(0)
    total = edge_coupling[pair, 0] * project(edge_inter[0, 0], lower[edge_local[pair, 0]])
    total += edge_coupling[pair, 1] * project(edge_inter[0, 1], upper[edge_local[pair, 1]])
    own = masked[0].astype(F32)
    partial[0] = integrals[0].astype(F32) + gap_matrix(virt, gap, pair) * own - total


def final_kernel(bucket, nbr, coupling, gap, masked, partial, virt, inter, *rest):
    terms, (named, residual, new_amps, partners, sems) = rest[:-5], rest[-5:]
    dev, _, _ = place()
    pair = pl.program_id(0)

    def partner_copy(index, entry):
        slot = slot_of(nbr[entry, 2 * dev + index // NBR] >> 1)
        return pltpu.make_async_copy(named.at[slot], partners.at[index], sems.at[index])

    @pl.when(pair == 0)
    def _():
        for index in range(2 * NBR):
            partner_copy(index, index % NBR).start()

    for entry in range(NBR):
        partner_copy(pair * NBR + entry, entry).wait()

    total = terms[0][0].astype(F32)
    for ref in terms[1:]:
        total += ref[0].astype(F32)
    for entry in range(NBR):
        total += coupling[pair, entry] * project(inter[0, entry], partners[pair * NBR + entry])
    keep = keep_square(jnp.left_shift(32, bucket[2 * dev + pair]))
    value = jnp.where(keep, partial[0] - total, 0.0)
    residual[0] = value
    change = value / gap_matrix(virt, gap, pair)
    new_amps[0] = jnp.where(keep, masked[0].astype(F32) - change, 0.0).astype(BF)


def local(
    amplitudes,
    integrals,
    virt_energy,
    pair_gap,
    rank_bucket,
    neighbours,
    intersection,
    coupling,
    edge_local,
    edge_intersection,
    edge_coupling,
):
    groups = lax.axis_size("grp")
    devices = lax.axis_size("dev")
    nbr = neighbours.T
    rows = [[y * COLS + x for x in range(COLS)] for y in range(ROWS)]

    def swap_columns(value):
        return lax.all_to_all(value, "dev", 0, 0, tiled=True, axis_index_groups=rows)

    def along_y(value, o):
        perm = [(i, (i + o * COLS) % devices) for i in range(devices)]
        return lax.ppermute(value, "dev", perm)

    block = jax.ShapeDtypeStruct((COLS * ROWS, R, R), BF)
    masked, outgoing = pl.pallas_call(
        return_kernel,
        grid=(2,),
        in_specs=[
            SMEM,
            SMEM,
            SMEM,
            pl.BlockSpec((1, R, R), lambda i: (i, 0, 0)),
            pl.BlockSpec((1, NBR, R, R), lambda i: (i, 0, 0, 0)),
        ],
        out_specs=[pl.BlockSpec((1, R, R), lambda i: (i, 0, 0)), ANY],
        out_shape=[jax.ShapeDtypeStruct((2, R, R), BF), block],
        scratch_shapes=[
            pltpu.VMEM((2 * NBR, R, R), BF),
            pltpu.SemaphoreType.DMA((2 * NBR,)),
        ],
        compiler_params=pltpu.CompilerParams(vmem_limit_bytes=LIMIT),
        name="returned_terms",
    )(rank_bucket, nbr, coupling, amplitudes, intersection)
    arrived = swap_columns(outgoing)
    params = pltpu.CompilerParams(vmem_limit_bytes=LIMIT)
    above2, below2 = along_y(masked, -2), along_y(masked, 2)
    above1, below1 = along_y(masked, -1), along_y(masked, 1)
    served = pl.pallas_call(
        served_kernel,
        in_specs=[SMEM],
        out_specs=SMEM,
        out_shape=jax.ShapeDtypeStruct((COLS * ROWS + 1,), jnp.int32),
        name="served_pairs",
    )(nbr)
    above3, below3 = along_y(above2, -1), along_y(below2, 1)
    above4, below4 = along_y(above2[:1], -2), along_y(below2[1:], 2)
    pieces = (masked, above1, below1, above2, below2, above3, below3, above4, below4)
    chosen = pl.pallas_call(
        select_kernel,
        in_specs=[SMEM] + [ANY] * (ROWS + 1),
        out_specs=ANY,
        out_shape=block,
        scratch_shapes=[
            pltpu.VMEM((2 * ROWS, R, R), BF),
            pltpu.SemaphoreType.DMA((ROWS + 1,)),
            pltpu.SemaphoreType.DMA((COLS * ROWS,)),
        ],
        compiler_params=params,
        name="named_pairs",
    )(served, *pieces)
    lower = lax.ppermute(masked, "grp", [(i, i + 1) for i in range(groups - 1)])
    upper = lax.ppermute(masked, "grp", [(i + 1, i) for i in range(groups - 1)])
    named = swap_columns(chosen)

    def pairs(count):
        return jax.ShapeDtypeStruct((count, R, R), BF)

    def column_terms(*groups):
        counts = [sum(len(sides) for _, sides in group) for group in groups]
        rows_in = COLS * sum(len(group) for group in groups)
        return pl.pallas_call(
            functools.partial(combine_kernel, groups),
            in_specs=[SMEM, ANY],
            out_specs=[VMEM] * len(groups),
            out_shape=[pairs(count) for count in counts],
            scratch_shapes=[
                pltpu.VMEM((rows_in, R, R), BF),
                pltpu.SemaphoreType.DMA((rows_in,)),
            ],
            compiler_params=params,
            name="column_terms",
        )(served, arrived)

    both = (0, 1)
    up, down, far_up, far_down = column_terms(
        ((1, both), (3, both)), ((-1, both), (-3, both)), ((4, (0,)),), ((4, (1,)),)
    )
    got_up, got_down = along_y(up, 1), along_y(down, -1)
    got_far_up, got_far_down = along_y(far_up, 2), along_y(far_down, -2)
    own, own_up, own_down = column_terms(((0, both),), ((2, both),), ((-2, both),))
    single = pl.BlockSpec((1, R, R), lambda i: (0, 0, 0))
    first = pl.BlockSpec((2, R, R), lambda i: (0, 0, 0))
    second = pl.BlockSpec((2, R, R), lambda i: (1, 0, 0))
    send_up, send_down = pl.pallas_call(
        fold_kernel,
        grid=(1,),
        in_specs=[second, second, single, single, first, first],
        out_specs=[first, first],
        out_shape=[pairs(2)] * 2,
        compiler_params=params,
        name="folded_terms",
    )(got_up, got_down, got_far_up, got_far_down, own_up, own_down)
    terms = [own, got_up, got_down, along_y(send_up, 2), along_y(send_down, -2)]
    each = pl.BlockSpec((1, R, R), lambda i: (i, 0, 0))

    def each_of(count):
        return pl.BlockSpec((1, count, R, R), lambda i: (i, 0, 0, 0))

    partial = pl.pallas_call(
        edge_kernel,
        grid=(2,),
        in_specs=[SMEM] * 3 + [each, each, VMEM, each_of(2), VMEM, VMEM],
        out_specs=each,
        out_shape=jax.ShapeDtypeStruct((2, R, R), F32),
        compiler_params=params,
        name="edges",
    )(
        edge_local,
        edge_coupling,
        pair_gap,
        masked,
        integrals,
        virt_energy,
        edge_intersection,
        lower,
        upper,
    )
    outputs = pl.pallas_call(
        final_kernel,
        grid=(2,),
        in_specs=[SMEM] * 4 + [each, each, VMEM, each_of(NBR)] + [each] * len(terms) + [ANY],
        out_specs=[each, each],
        out_shape=[
            jax.ShapeDtypeStruct((2, R, R), F32),
            jax.ShapeDtypeStruct((2, R, R), BF),
        ],
        scratch_shapes=[
            pltpu.VMEM((2 * NBR, R, R), BF),
            pltpu.SemaphoreType.DMA((2 * NBR,)),
        ],
        compiler_params=params,
        name="residual_update",
    )(
        rank_bucket,
        nbr,
        coupling,
        pair_gap,
        masked,
        partial,
        virt_energy,
        intersection,
        *terms,
        named,
    )
    return tuple(outputs)


def solution(mesh):
    pair = P(("grp", "dev"))
    placed = (pair, pair, pair, pair, P("grp"), P("grp")) + (pair,) * 5
    return jax.shard_map(
        local, mesh=mesh, in_specs=placed, out_specs=(pair, pair), check_vma=False
    )
```

time: 132 us -> 127 us (0.962)
  the two profiles are of different devices: /device:TPU:464 before, /device:TPU:1 now
where the time goes in v3:
time: 127 us; the launch traced here: 125 us
  starting transfers between devices  76.6 us (60%)
  Pallas kernels  27.8 us (22%)
  waiting for transfers between devices  14.9 us (12%)
  local copies, waits for them, and re-layouts  4.51 us (4%)
    ppermute x14, starting transfers between devices, along_y(): return lax.ppermute(value, 'dev', perm)  56.5 us
    ppermute x14, waiting for transfers between devices, along_y(): return lax.ppermute(value, 'dev', perm)  14.8 us
    all_to_all x2, starting transfers between devices, swap_columns(): lax.all_to_all(value, 'dev', 0, 0, tiled=True, axis_index_groups=rows)  9.89 us
    pallas_call x2, Pallas kernels, column_terms(): pl.pallas_call(functools.partial(combine_kernel, groups), in_specs=[SMEM,...  6.81 us
    ppermute x1, starting transfers between devices, local(): lower = lax.ppermute(masked, 'grp', [(i, i + 1) for i in range(groups - 1)])  5.84 us
    pallas_call x1, Pallas kernels, local(): pl.pallas_call(final_kernel, grid=(2,), in_specs=[SMEM] * 4 + [each, each...  5.56 us
    pallas_call x1, Pallas kernels, local(): pl.pallas_call(return_kernel, grid=(2,), in_specs=[SMEM, SMEM, SMEM, pl.B...  4.88 us
    unnamed x36, local copies, waits for them, and re-layouts  4.49 us
  transfers between devices with their start and end apart: 18, of which 5 were waited for; matrix products, arithmetic and copies ran while one was open for 0% of the time, Pallas kernels for 14%

profile of v3, /device:TPU:1, one launch (start us, length us, event | category | flops | bytes accessed | tf_op | source)
XLA Modules:
  0.0 124.8 jit_solution(12213417035934518206)
XLA Ops:
  0.6 4.9 %returned_terms.1 = (bf16[2,256,256]{2,1,0:T(8,128)(2,1)}, bf16[32,256,256]{2,1,0:T(8,128)(2,1)}) custom-call(s32[64]{0:T(128)} %bucket.3, s32[8,64]{1,0:T(8,128)} %bitcast.1, f32[2,8]{1,0:T(2,128)} %coupling.3, bf16[2,256,256]{2,1,0:T(8,128)(2,1)} %amps.1, bf16[2,8,256,256]{3,2,1,0:T(8,128)(2,1)} %inter.3), custom_call_target="tpu_custom_call" | custom-call | tf_op jit(solution)/shard_map/returned_terms/pallas_call | solution.py:249
  5.5 5.0 %all-to-all-start = ((bf16[32,256,256]{2,1,0:T(8,128)(2,1)}), bf16[32,256,256]{2,1,0:T(8,128)(2,1)}, u32[]{:S(2)}, u32[]{:S(2)}) async-start(bf16[32,256,256]{2,1,0:T(8,128)(2,1)} %get-tuple-element.14), calls=%async_computation | async-start | bytes 8388608 | tf_op jit(solution)/shard_map/all_to_all | solution.py:242
  10.5 5.1 %collective-permute-start.11 = (bf16[2,256,256]{2,1,0:T(8,128)(2,1)S(1)}, bf16[2,256,256]{2,1,0:T(8,128)(2,1)S(1)}, u32[]{:S(2)}, u32[]{:S(2)}) collective-permute-start(bf16[2,256,256]{2,1,0:T(8,128)(2,1)S(1)} %copy-done), channel_id=1, source_target_pairs={{0,8},{1,9},{2,10},{3,11},{4,12},{5,13},{6,14},{7,15},{8,16},{9,17... | collective-permute-start | bytes 786440 | tf_op jit(solution)/shard_map/ppermute | solution.py:246
  15.6 3.5 %collective-permute-start.10 = (bf16[2,256,256]{2,1,0:T(8,128)(2,1)S(1)}, bf16[2,256,256]{2,1,0:T(8,128)(2,1)S(1)}, u32[]{:S(2)}, u32[]{:S(2)}) collective-permute-start(bf16[2,256,256]{2,1,0:T(8,128)(2,1)S(1)} %copy-done), channel_id=1, source_target_pairs={{0,24},{1,25},{2,26},{3,27},{4,28},{5,29},{6,30},{7,31},{8,0},{9,1... | collective-permute-start | bytes 786440 | tf_op jit(solution)/shard_map/ppermute | solution.py:246
  22.0 3.7 %collective-permute-start.8 = (bf16[2,256,256]{2,1,0:T(8,128)(2,1)S(1)}, bf16[2,256,256]{2,1,0:T(8,128)(2,1)S(1)}, u32[]{:S(2)}, u32[]{:S(2)}) collective-permute-start(bf16[2,256,256]{2,1,0:T(8,128)(2,1)S(1)} %copy-done), channel_id=1, source_target_pairs={{0,28},{1,29},{2,30},{3,31},{4,0},{5,1},{6,2},{7,3},{8,4},{9,5},{1... | collective-permute-start | bytes 786440 | tf_op jit(solution)/shard_map/ppermute | solution.py:246
  25.7 4.7 %collective-permute-start.13 = (bf16[2,256,256]{2,1,0:T(8,128)(2,1)S(1)}, bf16[2,256,256]{2,1,0:T(8,128)(2,1)S(1)}, u32[]{:S(2)}, u32[]{:S(2)}) collective-permute-start(bf16[2,256,256]{2,1,0:T(8,128)(2,1)S(1)} %collective-permute-done.11.rest_4_), channel_id=1, source_target_pairs={{0,4},{1,5},{2,6},{3,7},{4,8},{5,9},{6,10},{7,11},{8,12},{9,13},{1... | collective-permute-start | bytes 786440 | tf_op jit(solution)/shard_map/ppermute | solution.py:246
  30.4 3.0 %collective-permute-done.10.rest_3_ = bf16[2,256,256]{2,1,0:T(8,128)(2,1)S(1)} collective-permute-done((bf16[2,256,256]{2,1,0:T(8,128)(2,1)S(1)}, bf16[2,256,256]{2,1,0:T(8,128)(2,1)S(1)}, u32[]{:S(2)}, u32[]{:S(2)}) %collective-permute-start.10) | collective-permute-done | bytes 262176 | tf_op jit(solution)/shard_map/ppermute | solution.py:246
  35.4 4.0 %collective-permute-start.15 = (bf16[1,256,256]{2,1,0:T(8,128)(2,1)S(1)}, bf16[1,256,256]{2,1,0:T(8,128)(2,1)S(1)}, u32[]{:S(2)}, u32[]{:S(2)}) collective-permute-start(bf16[1,256,256]{2,1,0:T(8,128)(2,1)S(1)} %slice.9), channel_id=1, source_target_pairs={{0,8},{1,9},{2,10},{3,11},{4,12},{5,13},{6,14},{7,15},{8,16},{9,17... | collective-permute-start | bytes 393224 | tf_op jit(solution)/shard_map/ppermute | solution.py:246
  39.4 3.4 %collective-permute-start.14 = (bf16[1,256,256]{2,1,0:T(8,128)(2,1)S(1)}, bf16[1,256,256]{2,1,0:T(8,128)(2,1)S(1)}, u32[]{:S(2)}, u32[]{:S(2)}) collective-permute-start(bf16[1,256,256]{2,1,0:T(8,128)(2,1)S(1)} %slice.8), channel_id=1, source_target_pairs={{0,24},{1,25},{2,26},{3,27},{4,28},{5,29},{6,30},{7,31},{8,0},{9,1... | collective-permute-start | bytes 393224 | tf_op jit(solution)/shard_map/ppermute | solution.py:246
  45.2 3.3 %collective-permute-done.14.rest_7_ = bf16[1,256,256]{2,1,0:T(8,128)(2,1)S(1)} collective-permute-done((bf16[1,256,256]{2,1,0:T(8,128)(2,1)S(1)}, bf16[1,256,256]{2,1,0:T(8,128)(2,1)S(1)}, u32[]{:S(2)}, u32[]{:S(2)}) %collective-permute-start.14) | collective-permute-done | bytes 131104 | tf_op jit(solution)/shard_map/ppermute | solution.py:246
  50.0 3.9 %named_pairs.1 = bf16[32,256,256]{2,1,0:T(8,128)(2,1)} custom-call(s32[33]{0:T(128)} %served_pairs.1.served, bf16[2,256,256]{2,1,0:T(8,128)(2,1)} %get-tuple-element.13.masked.rest_0_, bf16[2,256,256]{2,1,0:T(8,128)(2,1)} %copy-done.7, bf16[2,256,256]{2,1,0:T(8,128)(2,1)} %copy-done.6, bf16[2,256,256]{2,1,0:T(8,128)(2,1)} %copy-done.5, ...), custom_call_target="tpu_custom_call" | custom-call | tf_op jit(solution)/shard_map/named_pairs/pallas_call | solution.py:282
  53.9 4.9 %all-to-all-start.1 = ((bf16[32,256,256]{2,1,0:T(8,128)(2,1)}), bf16[32,256,256]{2,1,0:T(8,128)(2,1)}, u32[]{:S(2)}, u32[]{:S(2)}) async-start(bf16[32,256,256]{2,1,0:T(8,128)(2,1)} %named_pairs.1), calls=%async_computation.1 | async-start | bytes 8388608 | tf_op jit(solution)/shard_map/all_to_all | solution.py:242
  58.8 3.9 %column_terms.3 = (bf16[4,256,256]{2,1,0:T(8,128)(2,1)}, bf16[4,256,256]{2,1,0:T(8,128)(2,1)}, bf16[1,256,256]{2,1,0:T(8,128)(2,1)}, bf16[1,256,256]{2,1,0:T(8,128)(2,1)}) custom-call(s32[33]{0:T(128)} %served_pairs.1.served, bf16[32,256,256]{2,1,0:T(8,128)(2,1)} %all-to-all-done.arrived), custom_call_target="tpu_custom_call" | custom-call | tf_op jit(solution)/shard_map/column_terms/pallas_call | solution.py:305
  62.7 9.0 %collective-permute-start.2 = (bf16[4,256,256]{2,1,0:T(8,128)(2,1)}, bf16[4,256,256]{2,1,0:T(8,128)(2,1)S(1)}, u32[]{:S(2)}, u32[]{:S(2)}) collective-permute-start(bf16[4,256,256]{2,1,0:T(8,128)(2,1)} %get-tuple-element.16), channel_id=1, source_target_pairs={{0,4},{1,5},{2,6},{3,7},{4,8},{5,9},{6,10},{7,11},{8,12},{9,13},{1... | collective-permute-start | bytes 1572872 | tf_op jit(solution)/shard_map/ppermute | solution.py:246
  71.7 3.7 %collective-permute-start.3 = (bf16[4,256,256]{2,1,0:T(8,128)(2,1)}, bf16[4,256,256]{2,1,0:T(8,128)(2,1)S(1)}, u32[]{:S(2)}, u32[]{:S(2)}) collective-permute-start(bf16[4,256,256]{2,1,0:T(8,128)(2,1)} %get-tuple-element.17), channel_id=1, source_target_pairs={{0,28},{1,29},{2,30},{3,31},{4,0},{5,1},{6,2},{7,3},{8,4},{9,5},{1... | collective-permute-start | bytes 1572872 | tf_op jit(solution)/shard_map/ppermute | solution.py:246
  78.0 4.7 %collective-permute-start.5 = (bf16[1,256,256]{2,1,0:T(8,128)(2,1)}, bf16[1,256,256]{2,1,0:T(8,128)(2,1)S(1)}, u32[]{:S(2)}, u32[]{:S(2)}) collective-permute-start(bf16[1,256,256]{2,1,0:T(8,128)(2,1)} %get-tuple-element.19), channel_id=1, source_target_pairs={{0,24},{1,25},{2,26},{3,27},{4,28},{5,29},{6,30},{7,31},{8,0},{9,1... | collective-permute-start | bytes 393224 | tf_op jit(solution)/shard_map/ppermute | solution.py:246
  82.7 4.4 %collective-permute-start.1 = (bf16[2,256,256]{2,1,0:T(8,128)(2,1)S(1)}, bf16[2,256,256]{2,1,0:T(8,128)(2,1)S(1)}, u32[]{:S(2)}, u32[]{:S(2)}) collective-permute-start(bf16[2,256,256]{2,1,0:T(8,128)(2,1)S(1)} %copy-done.1), channel_id=1, source_target_pairs={{32,0},{64,32},{96,64},{128,96},{160,128},{192,160},{224,192},{256... | collective-permute-start | bytes 786440 | tf_op jit(solution)/shard_map/ppermute | solution.py:296
  87.1 3.0 %column_terms.2 = (bf16[2,256,256]{2,1,0:T(8,128)(2,1)}, bf16[2,256,256]{2,1,0:T(8,128)(2,1)}, bf16[2,256,256]{2,1,0:T(8,128)(2,1)}) custom-call(s32[33]{0:T(128)} %served_pairs.1.served, bf16[32,256,256]{2,1,0:T(8,128)(2,1)} %all-to-all-done.arrived), custom_call_target="tpu_custom_call" | custom-call | tf_op jit(solution)/shard_map/column_terms/pallas_call | solution.py:305
  90.1 5.8 %collective-permute-start = (bf16[2,256,256]{2,1,0:T(8,128)(2,1)S(1)}, bf16[2,256,256]{2,1,0:T(8,128)(2,1)S(1)}, u32[]{:S(2)}, u32[]{:S(2)}) collective-permute-start(bf16[2,256,256]{2,1,0:T(8,128)(2,1)S(1)} %copy-done.1), channel_id=1, source_target_pairs={{0,32},{32,64},{64,96},{96,128},{128,160},{160,192},{192,224},{224... | collective-permute-start | bytes 786440 | tf_op jit(solution)/shard_map/ppermute | solution.py:295
  99.2 2.8 %collective-permute-start.6 = (bf16[2,256,256]{2,1,0:T(8,128)(2,1)}, bf16[2,256,256]{2,1,0:T(8,128)(2,1)S(1)}, u32[]{:S(2)}, u32[]{:S(2)}) collective-permute-start(bf16[2,256,256]{2,1,0:T(8,128)(2,1)} %get-tuple-element.22), channel_id=1, source_target_pairs={{0,8},{1,9},{2,10},{3,11},{4,12},{5,13},{6,14},{7,15},{8,16},{9,17... | collective-permute-start | bytes 786440 | tf_op jit(solution)/shard_map/ppermute | solution.py:246
  102.0 4.6 %collective-permute-start.7 = (bf16[2,256,256]{2,1,0:T(8,128)(2,1)}, bf16[2,256,256]{2,1,0:T(8,128)(2,1)S(1)}, u32[]{:S(2)}, u32[]{:S(2)}) collective-permute-start(bf16[2,256,256]{2,1,0:T(8,128)(2,1)} %get-tuple-element.23), channel_id=1, source_target_pairs={{0,24},{1,25},{2,26},{3,27},{4,28},{5,29},{6,30},{7,31},{8,0},{9,1... | collective-permute-start | bytes 786440 | tf_op jit(solution)/shard_map/ppermute | solution.py:246
  108.0 2.9 %edges.1.partial = f32[2,256,256]{2,1,0:T(8,128)} custom-call(s32[2,2]{1,0:T(2,128)} %edge_local.1, f32[2,2]{1,0:T(2,128)} %edge_coupling.1, f32[2]{0:T(128)} %gap.3, bf16[2,256,256]{2,1,0:T(8,128)(2,1)} %get-tuple-element.13.masked.rest_0_, bf16[2,256,256]{2,1,0:T(8,128)(2,1)} %integrals.1, f32[2,256]{1,0:T(2,128)} %virt.3, ...), custom_call_target="tpu_custom_call" | custom-call | tf_op jit(solution)/shard_map/edges/pallas_call | solution.py:343
  112.3 6.3 %collective-permute-done.7.rest_4_ = bf16[2,256,256]{2,1,0:T(8,128)(2,1)S(1)} collective-permute-done((bf16[2,256,256]{2,1,0:T(8,128)(2,1)}, bf16[2,256,256]{2,1,0:T(8,128)(2,1)S(1)}, u32[]{:S(2)}, u32[]{:S(2)}) %collective-permute-start.7) | collective-permute-done | bytes 262176 | tf_op jit(solution)/shard_map/ppermute | solution.py:246
  119.3 5.6 %residual_update.1 = (f32[2,256,256]{2,1,0:T(8,128)}, bf16[2,256,256]{2,1,0:T(8,128)(2,1)}) custom-call(s32[64]{0:T(128)} %bucket.3, s32[8,64]{1,0:T(8,128)} %bitcast.3, f32[2,8]{1,0:T(2,128)} %coupling.3, f32[2]{0:T(128)} %gap.3, bf16[2,256,256]{2,1,0:T(8,128)(2,1)} %get-tuple-element.13.masked.rest_0_, f32[2,256,256]{2,1,0:T(8,128)} %edges.1.partial, ...), custom_call_target="tpu_custom_call" | custom-call | tf_op jit(solution)/shard_map/residual_update/pallas_call | solution.py:362
  (58 shorter events, 17.9 us)
Async XLA Ops:
  5.5 48.4 %all-to-all-start = ((bf16[32,256,256]{2,1,0:T(8,128)(2,1)}), bf16[32,256,256]{2,1,0:T(8,128)(2,1)}, u32[]{:S(2)}, u32[]{:S(2)}) async-start(bf16[32,256,256]{2,1,0:T(8,128)(2,1)} %get-tuple-element.14), calls=%async_computation | async-start | bytes 8388608 | tf_op jit(solution)/shard_map/all_to_all | solution.py:242
  10.5 15.1 %collective-permute-start.11 = (bf16[2,256,256]{2,1,0:T(8,128)(2,1)S(1)}, bf16[2,256,256]{2,1,0:T(8,128)(2,1)S(1)}, u32[]{:S(2)}, u32[]{:S(2)}) collective-permute-start(bf16[2,256,256]{2,1,0:T(8,128)(2,1)S(1)} %copy-done), channel_id=1, source_target_pairs={{0,8},{1,9},{2,10},{3,11},{4,12},{5,13},{6,14},{7,15},{8,16},{9,17... | collective-permute-start | bytes 786440 | tf_op jit(solution)/shard_map/ppermute | solution.py:246
  15.6 17.8 %collective-permute-start.10 = (bf16[2,256,256]{2,1,0:T(8,128)(2,1)S(1)}, bf16[2,256,256]{2,1,0:T(8,128)(2,1)S(1)}, u32[]{:S(2)}, u32[]{:S(2)}) collective-permute-start(bf16[2,256,256]{2,1,0:T(8,128)(2,1)S(1)} %copy-done), channel_id=1, source_target_pairs={{0,24},{1,25},{2,26},{3,27},{4,28},{5,29},{6,30},{7,31},{8,0},{9,1... | collective-permute-start | bytes 786440 | tf_op jit(solution)/shard_map/ppermute | solution.py:246
  19.2 20.2 %collective-permute-start.9 = (bf16[2,256,256]{2,1,0:T(8,128)(2,1)S(1)}, bf16[2,256,256]{2,1,0:T(8,128)(2,1)S(1)}, u32[]{:S(2)}, u32[]{:S(2)}) collective-permute-start(bf16[2,256,256]{2,1,0:T(8,128)(2,1)S(1)} %copy-done), channel_id=1, source_target_pairs={{0,4},{1,5},{2,6},{3,7},{4,8},{5,9},{6,10},{7,11},{8,12},{9,13},{1... | collective-permute-start | bytes 786440 | tf_op jit(solution)/shard_map/ppermute | solution.py:246
  22.0 22.3 %collective-permute-start.8 = (bf16[2,256,256]{2,1,0:T(8,128)(2,1)S(1)}, bf16[2,256,256]{2,1,0:T(8,128)(2,1)S(1)}, u32[]{:S(2)}, u32[]{:S(2)}) collective-permute-start(bf16[2,256,256]{2,1,0:T(8,128)(2,1)S(1)} %copy-done), channel_id=1, source_target_pairs={{0,28},{1,29},{2,30},{3,31},{4,0},{5,1},{6,2},{7,3},{8,4},{9,5},{1... | collective-permute-start | bytes 786440 | tf_op jit(solution)/shard_map/ppermute | solution.py:246
  25.7 22.8 %copy-start.4 = (bf16[2,256,256]{2,1,0:T(8,128)(2,1)}, bf16[2,256,256]{2,1,0:T(8,128)(2,1)S(1)}, u32[]{:S(2)}) copy-start(bf16[2,256,256]{2,1,0:T(8,128)(2,1)S(1)} %collective-permute-done.11.rest_4_) | copy-start | bytes 786436
  25.7 22.8 %collective-permute-start.13 = (bf16[2,256,256]{2,1,0:T(8,128)(2,1)S(1)}, bf16[2,256,256]{2,1,0:T(8,128)(2,1)S(1)}, u32[]{:S(2)}, u32[]{:S(2)}) collective-permute-start(bf16[2,256,256]{2,1,0:T(8,128)(2,1)S(1)} %collective-permute-done.11.rest_4_), channel_id=1, source_target_pairs={{0,4},{1,5},{2,6},{3,7},{4,8},{5,9},{6,10},{7,11},{8,12},{9,13},{1... | collective-permute-start | bytes 786440 | tf_op jit(solution)/shard_map/ppermute | solution.py:246
  33.4 15.1 %copy-start.5 = (bf16[2,256,256]{2,1,0:T(8,128)(2,1)}, bf16[2,256,256]{2,1,0:T(8,128)(2,1)S(1)}, u32[]{:S(2)}) copy-start(bf16[2,256,256]{2,1,0:T(8,128)(2,1)S(1)} %collective-permute-done.10.rest_3_) | copy-start | bytes 786436
  33.4 15.1 %collective-permute-start.12 = (bf16[2,256,256]{2,1,0:T(8,128)(2,1)S(1)}, bf16[2,256,256]{2,1,0:T(8,128)(2,1)S(1)}, u32[]{:S(2)}, u32[]{:S(2)}) collective-permute-start(bf16[2,256,256]{2,1,0:T(8,128)(2,1)S(1)} %collective-permute-done.10.rest_3_), channel_id=1, source_target_pairs={{0,28},{1,29},{2,30},{3,31},{4,0},{5,1},{6,2},{7,3},{8,4},{9,5},{1... | collective-permute-start | bytes 786440 | tf_op jit(solution)/shard_map/ppermute | solution.py:246
  35.4 9.9 %collective-permute-start.15 = (bf16[1,256,256]{2,1,0:T(8,128)(2,1)S(1)}, bf16[1,256,256]{2,1,0:T(8,128)(2,1)S(1)}, u32[]{:S(2)}, u32[]{:S(2)}) collective-permute-start(bf16[1,256,256]{2,1,0:T(8,128)(2,1)S(1)} %slice.9), channel_id=1, source_target_pairs={{0,8},{1,9},{2,10},{3,11},{4,12},{5,13},{6,14},{7,15},{8,16},{9,17... | collective-permute-start | bytes 393224 | tf_op jit(solution)/shard_map/ppermute | solution.py:246
  39.4 9.2 %copy-start.6 = (bf16[2,256,256]{2,1,0:T(8,128)(2,1)}, bf16[2,256,256]{2,1,0:T(8,128)(2,1)S(1)}, u32[]{:S(2)}) copy-start(bf16[2,256,256]{2,1,0:T(8,128)(2,1)S(1)} %collective-permute-done.9.rest_2_) | copy-start | bytes 786436
  39.4 9.1 %collective-permute-start.14 = (bf16[1,256,256]{2,1,0:T(8,128)(2,1)S(1)}, bf16[1,256,256]{2,1,0:T(8,128)(2,1)S(1)}, u32[]{:S(2)}, u32[]{:S(2)}) collective-permute-start(bf16[1,256,256]{2,1,0:T(8,128)(2,1)S(1)} %slice.8), channel_id=1, source_target_pairs={{0,24},{1,25},{2,26},{3,27},{4,28},{5,29},{6,30},{7,31},{8,0},{9,1... | collective-permute-start | bytes 393224 | tf_op jit(solution)/shard_map/ppermute | solution.py:246
  53.9 57.0 %all-to-all-start.1 = ((bf16[32,256,256]{2,1,0:T(8,128)(2,1)}), bf16[32,256,256]{2,1,0:T(8,128)(2,1)}, u32[]{:S(2)}, u32[]{:S(2)}) async-start(bf16[32,256,256]{2,1,0:T(8,128)(2,1)} %named_pairs.1), calls=%async_computation.1 | async-start | bytes 8388608 | tf_op jit(solution)/shard_map/all_to_all | solution.py:242
  58.8 23.9 %copy-start.1 = (bf16[2,256,256]{2,1,0:T(8,128)(2,1)S(1)}, bf16[2,256,256]{2,1,0:T(8,128)(2,1)}, u32[]{:S(2)}) copy-start(bf16[2,256,256]{2,1,0:T(8,128)(2,1)} %get-tuple-element.13.masked.rest_0_) | copy-start | bytes 786436
  62.7 33.3 %collective-permute-start.2 = (bf16[4,256,256]{2,1,0:T(8,128)(2,1)}, bf16[4,256,256]{2,1,0:T(8,128)(2,1)S(1)}, u32[]{:S(2)}, u32[]{:S(2)}) collective-permute-start(bf16[4,256,256]{2,1,0:T(8,128)(2,1)} %get-tuple-element.16), channel_id=1, source_target_pairs={{0,4},{1,5},{2,6},{3,7},{4,8},{5,9},{6,10},{7,11},{8,12},{9,13},{1... | collective-permute-start | bytes 1572872 | tf_op jit(solution)/shard_map/ppermute | solution.py:246
  71.7 24.4 %collective-permute-start.3 = (bf16[4,256,256]{2,1,0:T(8,128)(2,1)}, bf16[4,256,256]{2,1,0:T(8,128)(2,1)S(1)}, u32[]{:S(2)}, u32[]{:S(2)}) collective-permute-start(bf16[4,256,256]{2,1,0:T(8,128)(2,1)} %get-tuple-element.17), channel_id=1, source_target_pairs={{0,28},{1,29},{2,30},{3,31},{4,0},{5,1},{6,2},{7,3},{8,4},{9,5},{1... | collective-permute-start | bytes 1572872 | tf_op jit(solution)/shard_map/ppermute | solution.py:246
  75.3 14.8 %collective-permute-start.4 = (bf16[1,256,256]{2,1,0:T(8,128)(2,1)}, bf16[1,256,256]{2,1,0:T(8,128)(2,1)S(1)}, u32[]{:S(2)}, u32[]{:S(2)}) collective-permute-start(bf16[1,256,256]{2,1,0:T(8,128)(2,1)} %get-tuple-element.18), channel_id=1, source_target_pairs={{0,8},{1,9},{2,10},{3,11},{4,12},{5,13},{6,14},{7,15},{8,16},{9,17... | collective-permute-start | bytes 393224 | tf_op jit(solution)/shard_map/ppermute | solution.py:246
  78.0 17.9 %collective-permute-start.5 = (bf16[1,256,256]{2,1,0:T(8,128)(2,1)}, bf16[1,256,256]{2,1,0:T(8,128)(2,1)S(1)}, u32[]{:S(2)}, u32[]{:S(2)}) collective-permute-start(bf16[1,256,256]{2,1,0:T(8,128)(2,1)} %get-tuple-element.19), channel_id=1, source_target_pairs={{0,24},{1,25},{2,26},{3,27},{4,28},{5,29},{6,30},{7,31},{8,0},{9,1... | collective-permute-start | bytes 393224 | tf_op jit(solution)/shard_map/ppermute | solution.py:246
  82.7 23.9 %collective-permute-start.1 = (bf16[2,256,256]{2,1,0:T(8,128)(2,1)S(1)}, bf16[2,256,256]{2,1,0:T(8,128)(2,1)S(1)}, u32[]{:S(2)}, u32[]{:S(2)}) collective-permute-start(bf16[2,256,256]{2,1,0:T(8,128)(2,1)S(1)} %copy-done.1), channel_id=1, source_target_pairs={{32,0},{64,32},{96,64},{128,96},{160,128},{192,160},{224,192},{256... | collective-permute-start | bytes 786440 | tf_op jit(solution)/shard_map/ppermute | solution.py:296
  90.1 5.9 %copy-start.14 = (bf16[1,256,256]{2,1,0:T(8,128)(2,1)}, bf16[1,256,256]{2,1,0:T(8,128)(2,1)S(1)}, u32[]{:S(2)}) copy-start(bf16[1,256,256]{2,1,0:T(8,128)(2,1)S(1)} %collective-permute-done.4.far_up) | copy-start | bytes 393220
  90.1 16.5 %collective-permute-start = (bf16[2,256,256]{2,1,0:T(8,128)(2,1)S(1)}, bf16[2,256,256]{2,1,0:T(8,128)(2,1)S(1)}, u32[]{:S(2)}, u32[]{:S(2)}) collective-permute-start(bf16[2,256,256]{2,1,0:T(8,128)(2,1)S(1)} %copy-done.1), channel_id=1, source_target_pairs={{0,32},{32,64},{64,96},{96,128},{128,160},{160,192},{192,224},{224... | collective-permute-start | bytes 786440 | tf_op jit(solution)/shard_map/ppermute | solution.py:295
  99.2 13.1 %collective-permute-start.6 = (bf16[2,256,256]{2,1,0:T(8,128)(2,1)}, bf16[2,256,256]{2,1,0:T(8,128)(2,1)S(1)}, u32[]{:S(2)}, u32[]{:S(2)}) collective-permute-start(bf16[2,256,256]{2,1,0:T(8,128)(2,1)} %get-tuple-element.22), channel_id=1, source_target_pairs={{0,8},{1,9},{2,10},{3,11},{4,12},{5,13},{6,14},{7,15},{8,16},{9,17... | collective-permute-start | bytes 786440 | tf_op jit(solution)/shard_map/ppermute | solution.py:246
  102.0 16.5 %collective-permute-start.7 = (bf16[2,256,256]{2,1,0:T(8,128)(2,1)}, bf16[2,256,256]{2,1,0:T(8,128)(2,1)S(1)}, u32[]{:S(2)}, u32[]{:S(2)}) collective-permute-start(bf16[2,256,256]{2,1,0:T(8,128)(2,1)} %get-tuple-element.23), channel_id=1, source_target_pairs={{0,24},{1,25},{2,26},{3,27},{4,28},{5,29},{6,30},{7,31},{8,0},{9,1... | collective-permute-start | bytes 786440 | tf_op jit(solution)/shard_map/ppermute | solution.py:246
  112.3 6.3 %copy-start.12 = (bf16[2,256,256]{2,1,0:T(8,128)(2,1)}, bf16[2,256,256]{2,1,0:T(8,128)(2,1)S(1)}, u32[]{:S(2)}) copy-start(bf16[2,256,256]{2,1,0:T(8,128)(2,1)S(1)} %collective-permute-done.6.rest_3_) | copy-start | bytes 786436
  (12 other events, 19.3 us)

commit v4 on v3

--- a/solution.py
+++ b/solution.py
@@ -51,10 +51,14 @@
     rank = jnp.left_shift(32, bucket[2 * dev + pair])
     own = jnp.where(keep_square(rank), amps[0].astype(F32), 0.0).astype(BF)
     masked[0] = own
+    halves = []
     for entry in range(NBR):
-        s = inter[0, entry]
-        half = lax.dot_general(s, own, (((0,), (0,)), ((), ())), preferred_element_type=F32)
-        term = jnp.dot(half.astype(BF), s, preferred_element_type=F32)
+        half = lax.dot_general(
+            inter[0, entry], own, (((0,), (0,)), ((), ())), preferred_element_type=F32
+        )
+        halves.append(half.astype(BF))
+    for entry in range(NBR):
+        term = jnp.dot(halves[entry], inter[0, entry], preferred_element_type=F32)
         terms[pair * NBR + entry] = (coupling[pair, entry] * term).astype(BF)
     for entry in range(NBR):
         copy(pair, entry).start()
@@ -279,6 +283,9 @@
     above3, below3 = along_y(above2, -1), along_y(below2, 1)
     above4, below4 = along_y(above2[:1], -2), along_y(below2[1:], 2)
     pieces = (masked, above1, below1, above2, below2, above3, below3, above4, below4)
+    lower = lax.ppermute(masked, "grp", [(i, i + 1) for i in range(groups - 1)])
+    upper = lax.ppermute(masked, "grp", [(i + 1, i) for i in range(groups - 1)])
+    served, lower, upper = lax.optimization_barrier((served, lower, upper))
     chosen = pl.pallas_call(
         select_kernel,
         in_specs=[SMEM] + [ANY] * (ROWS + 1),
@@ -292,8 +299,6 @@
         compiler_params=params,
         name="named_pairs",
     )(served, *pieces)
-    lower = lax.ppermute(masked, "grp", [(i, i + 1) for i in range(groups - 1)])
-    upper = lax.ppermute(masked, "grp", [(i + 1, i) for i in range(groups - 1)])
     named = swap_columns(chosen)
 
     def pairs(count):
@@ -311,7 +316,7 @@
                 pltpu.VMEM((rows_in, R, R), BF),
                 pltpu.SemaphoreType.DMA((rows_in,)),
             ],
-            compiler_params=params,
+            compiler_params=pltpu.CompilerParams(vmem_limit_bytes=16 << 20),
             name="column_terms",
         )(served, arrived)
 
@@ -331,7 +336,7 @@
         in_specs=[second, second, single, single, first, first],
         out_specs=[first, first],
         out_shape=[pairs(2)] * 2,
-        compiler_params=params,
+        compiler_params=pltpu.CompilerParams(vmem_limit_bytes=12 << 20),
         name="folded_terms",
     )(got_up, got_down, got_far_up, got_far_down, own_up, own_down)
     terms = [own, got_up, got_down, along_y(send_up, 2), along_y(send_down, -2)]

time: 127 us -> 123 us (0.969)
  waiting for transfers between devices: 14.9 us -> 21.5 us
  starting transfers between devices: 76.6 us -> 71.1 us
  Pallas kernels: 27.8 us -> 23.9 us
  local copies, waits for them, and re-layouts: 4.51 us -> 2.94 us
    all_to_all x2, waiting for transfers between devices: 0.01 us -> 13.1 us  [swap_columns(): lax.all_to_all(value, 'dev', 0, 0, tiled=True, axis_index_groups=rows)]
    ppermute x14, waiting for transfers between devices: 14.8 us -> 8.38 us  [along_y(): return lax.ppermute(value, 'dev', perm)]
    ppermute x14, starting transfers between devices: 56.5 us -> 52 us  [along_y(): return lax.ppermute(value, 'dev', perm)]
    ppermute x1, starting transfers between devices: 5.84 us -> 1.92 us  [local(): lower = lax.ppermute(masked, 'grp', [(i, i + 1) for i in range(groups - 1)])]
    ppermute x1, starting transfers between devices: 4.38 us -> 7.32 us  [local(): upper = lax.ppermute(masked, 'grp', [(i + 1, i) for i in range(groups - 1)])]
    pallas_call x1, Pallas kernels: 2.21 us -> 0.16 us  [local(): pl.pallas_call(fold_kernel, grid=(1,), in_specs=[second, second, single,...]
    pallas_call x2, Pallas kernels: 6.81 us -> 5.05 us  [column_terms(): pl.pallas_call(functools.partial(combine_kernel, groups), in_specs=[SMEM,...]
    unnamed x36 -> x34, local copies, waits for them, and re-layouts: 4.49 us -> 2.92 us
  transfers between devices with their start and end apart: 18 -> 18, of which waited for: 5 -> 5; matrix products, arithmetic and copies ran while one was open for 0% -> 0% of each run, Pallas kernels for 14% -> 11%
where the time goes in v4:
time: 123 us; the launch traced here: 121 us
  starting transfers between devices  71.1 us (58%)
  Pallas kernels  23.9 us (19%)
  waiting for transfers between devices  21.5 us (17%)
  local copies, waits for them, and re-layouts  2.94 us (2%)
    ppermute x14, starting transfers between devices, along_y(): return lax.ppermute(value, 'dev', perm)  52 us
    all_to_all x2, waiting for transfers between devices, swap_columns(): lax.all_to_all(value, 'dev', 0, 0, tiled=True, axis_index_groups=rows)  13.1 us
    all_to_all x2, starting transfers between devices, swap_columns(): lax.all_to_all(value, 'dev', 0, 0, tiled=True, axis_index_groups=rows)  9.89 us
    ppermute x14, waiting for transfers between devices, along_y(): return lax.ppermute(value, 'dev', perm)  8.38 us
    ppermute x1, starting transfers between devices, local(): upper = lax.ppermute(masked, 'grp', [(i + 1, i) for i in range(groups - 1)])  7.32 us
    pallas_call x1, Pallas kernels, local(): pl.pallas_call(final_kernel, grid=(2,), in_specs=[SMEM] * 4 + [each, each...  5.56 us
    pallas_call x2, Pallas kernels, column_terms(): pl.pallas_call(functools.partial(combine_kernel, groups), in_specs=[SMEM,...  5.05 us
    pallas_call x1, Pallas kernels, local(): pl.pallas_call(return_kernel, grid=(2,), in_specs=[SMEM, SMEM, SMEM, pl.B...  4.77 us
  transfers between devices with their start and end apart: 18, of which 5 were waited for; matrix products, arithmetic and copies ran while one was open for 0% of the time, Pallas kernels for 11%

profile of v4, /device:TPU:1, one launch (start us, length us, event | category | flops | bytes accessed | tf_op | source)
XLA Modules:
  0.0 120.5 jit_solution(11770078298781604061)
XLA Ops:
  0.6 4.8 %returned_terms.1 = (bf16[2,256,256]{2,1,0:T(8,128)(2,1)}, bf16[32,256,256]{2,1,0:T(8,128)(2,1)}) custom-call(s32[64]{0:T(128)} %bucket.3, s32[8,64]{1,0:T(8,128)} %bitcast.1, f32[2,8]{1,0:T(2,128)} %coupling.3, bf16[2,256,256]{2,1,0:T(8,128)(2,1)} %amps.1, bf16[2,8,256,256]{3,2,1,0:T(8,128)(2,1)} %inter.3), custom_call_target="tpu_custom_call" | custom-call | tf_op jit(solution)/shard_map/returned_terms/pallas_call | solution.py:253
  5.4 5.0 %all-to-all-start = ((bf16[32,256,256]{2,1,0:T(8,128)(2,1)}), bf16[32,256,256]{2,1,0:T(8,128)(2,1)}, u32[]{:S(2)}, u32[]{:S(2)}) async-start(bf16[32,256,256]{2,1,0:T(8,128)(2,1)} %get-tuple-element.20), calls=%async_computation | async-start | bytes 8388608 | tf_op jit(solution)/shard_map/all_to_all | solution.py:246
  10.4 5.0 %collective-permute-start.11 = (bf16[2,256,256]{2,1,0:T(8,128)(2,1)S(1)}, bf16[2,256,256]{2,1,0:T(8,128)(2,1)S(1)}, u32[]{:S(2)}, u32[]{:S(2)}) collective-permute-start(bf16[2,256,256]{2,1,0:T(8,128)(2,1)S(1)} %copy-done.4), channel_id=1, source_target_pairs={{0,8},{1,9},{2,10},{3,11},{4,12},{5,13},{6,14},{7,15},{8,16},{9,17... | collective-permute-start | bytes 786440 | tf_op jit(solution)/shard_map/ppermute | solution.py:250
  15.4 3.6 %collective-permute-start.10 = (bf16[2,256,256]{2,1,0:T(8,128)(2,1)S(1)}, bf16[2,256,256]{2,1,0:T(8,128)(2,1)S(1)}, u32[]{:S(2)}, u32[]{:S(2)}) collective-permute-start(bf16[2,256,256]{2,1,0:T(8,128)(2,1)S(1)} %copy-done.4), channel_id=1, source_target_pairs={{0,24},{1,25},{2,26},{3,27},{4,28},{5,29},{6,30},{7,31},{8,0},{9,1... | collective-permute-start | bytes 786440 | tf_op jit(solution)/shard_map/ppermute | solution.py:250
  19.0 2.8 %collective-permute-start.9 = (bf16[2,256,256]{2,1,0:T(8,128)(2,1)S(1)}, bf16[2,256,256]{2,1,0:T(8,128)(2,1)S(1)}, u32[]{:S(2)}, u32[]{:S(2)}) collective-permute-start(bf16[2,256,256]{2,1,0:T(8,128)(2,1)S(1)} %copy-done.4), channel_id=1, source_target_pairs={{0,4},{1,5},{2,6},{3,7},{4,8},{5,9},{6,10},{7,11},{8,12},{9,13},{1... | collective-permute-start | bytes 786440 | tf_op jit(solution)/shard_map/ppermute | solution.py:250
  21.8 7.3 %collective-permute-start.1 = (bf16[2,256,256]{2,1,0:T(8,128)(2,1)S(1)}, bf16[2,256,256]{2,1,0:T(8,128)(2,1)S(1)}, u32[]{:S(2)}, u32[]{:S(2)}) collective-permute-start(bf16[2,256,256]{2,1,0:T(8,128)(2,1)S(1)} %copy-done.4), channel_id=1, source_target_pairs={{32,0},{64,32},{96,64},{128,96},{160,128},{192,160},{224,192},{256... | collective-permute-start | bytes 786440 | tf_op jit(solution)/shard_map/ppermute | solution.py:287
  31.1 4.9 %collective-permute-start.8 = (bf16[2,256,256]{2,1,0:T(8,128)(2,1)S(1)}, bf16[2,256,256]{2,1,0:T(8,128)(2,1)S(1)}, u32[]{:S(2)}, u32[]{:S(2)}) collective-permute-start(bf16[2,256,256]{2,1,0:T(8,128)(2,1)S(1)} %copy-done.4), channel_id=1, source_target_pairs={{0,28},{1,29},{2,30},{3,31},{4,0},{5,1},{6,2},{7,3},{8,4},{9,5},{1... | collective-permute-start | bytes 786440 | tf_op jit(solution)/shard_map/ppermute | solution.py:250
  37.9 4.6 %collective-permute-start.12 = (bf16[2,256,256]{2,1,0:T(8,128)(2,1)S(1)}, bf16[2,256,256]{2,1,0:T(8,128)(2,1)S(1)}, u32[]{:S(2)}, u32[]{:S(2)}) collective-permute-start(bf16[2,256,256]{2,1,0:T(8,128)(2,1)S(1)} %collective-permute-done.10.rest_3_), channel_id=1, source_target_pairs={{0,28},{1,29},{2,30},{3,31},{4,0},{5,1},{6,2},{7,3},{8,4},{9,5},{1... | collective-permute-start | bytes 786440 | tf_op jit(solution)/shard_map/ppermute | solution.py:250
  44.5 5.5 %collective-permute-start.14 = (bf16[1,256,256]{2,1,0:T(8,128)(2,1)S(1)}, bf16[1,256,256]{2,1,0:T(8,128)(2,1)S(1)}, u32[]{:S(2)}, u32[]{:S(2)}) collective-permute-start(bf16[1,256,256]{2,1,0:T(8,128)(2,1)S(1)} %slice.8), channel_id=1, source_target_pairs={{0,24},{1,25},{2,26},{3,27},{4,28},{5,29},{6,30},{7,31},{8,0},{9,1... | collective-permute-start | bytes 393224 | tf_op jit(solution)/shard_map/ppermute | solution.py:250
  51.5 2.8 %collective-permute-done.15.rest_8_ = bf16[1,256,256]{2,1,0:T(8,128)(2,1)S(1)} collective-permute-done((bf16[1,256,256]{2,1,0:T(8,128)(2,1)S(1)}, bf16[1,256,256]{2,1,0:T(8,128)(2,1)S(1)}, u32[]{:S(2)}, u32[]{:S(2)}) %collective-permute-start.15) | collective-permute-done | bytes 131104 | tf_op jit(solution)/shard_map/ppermute | solution.py:250
  56.7 3.9 %named_pairs.1 = bf16[32,256,256]{2,1,0:T(8,128)(2,1)} custom-call(s32[33]{0:T(128)} %served_pairs.1.served, bf16[2,256,256]{2,1,0:T(8,128)(2,1)} %get-tuple-element.16.masked.rest_0_, bf16[2,256,256]{2,1,0:T(8,128)(2,1)} %copy-done.10, bf16[2,256,256]{2,1,0:T(8,128)(2,1)} %copy-done.9, bf16[2,256,256]{2,1,0:T(8,128)(2,1)} %copy-done.6, ...), custom_call_target="tpu_custom_call" | custom-call | tf_op jit(solution)/shard_map/named_pairs/pallas_call | solution.py:289
  60.7 4.9 %all-to-all-start.1 = ((bf16[32,256,256]{2,1,0:T(8,128)(2,1)}), bf16[32,256,256]{2,1,0:T(8,128)(2,1)}, u32[]{:S(2)}, u32[]{:S(2)}) async-start(bf16[32,256,256]{2,1,0:T(8,128)(2,1)} %named_pairs.1), calls=%async_computation.1 | async-start | bytes 8388608 | tf_op jit(solution)/shard_map/all_to_all | solution.py:246
  65.6 2.8 %column_terms.3 = (bf16[4,256,256]{2,1,0:T(8,128)(2,1)S(1)}, bf16[4,256,256]{2,1,0:T(8,128)(2,1)S(1)}, bf16[1,256,256]{2,1,0:T(8,128)(2,1)S(1)}, bf16[1,256,256]{2,1,0:T(8,128)(2,1)S(1)}) custom-call(s32[33]{0:T(128)S(1)} %copy-done.3, bf16[32,256,256]{2,1,0:T(8,128)(2,1)} %all-to-all-done.arrived), custom_call_target="tpu_custom_call" | custom-call | tf_op jit(solution)/shard_map/column_terms/pallas_call | solution.py:310
  68.4 2.0 %collective-permute-start.2 = (bf16[4,256,256]{2,1,0:T(8,128)(2,1)S(1)}, bf16[4,256,256]{2,1,0:T(8,128)(2,1)S(1)}, u32[]{:S(2)}, u32[]{:S(2)}) collective-permute-start(bf16[4,256,256]{2,1,0:T(8,128)(2,1)S(1)} %get-tuple-element.22), channel_id=1, source_target_pairs={{0,4},{1,5},{2,6},{3,7},{4,8},{5,9},{6,10},{7,11},{8,12},{9,13},{1... | collective-permute-start | bytes 1572872 | tf_op jit(solution)/shard_map/ppermute | solution.py:250
  70.4 4.5 %collective-permute-start.3 = (bf16[4,256,256]{2,1,0:T(8,128)(2,1)S(1)}, bf16[4,256,256]{2,1,0:T(8,128)(2,1)S(1)}, u32[]{:S(2)}, u32[]{:S(2)}) collective-permute-start(bf16[4,256,256]{2,1,0:T(8,128)(2,1)S(1)} %get-tuple-element.23), channel_id=1, source_target_pairs={{0,28},{1,29},{2,30},{3,31},{4,0},{5,1},{6,2},{7,3},{8,4},{9,5},{1... | collective-permute-start | bytes 1572872 | tf_op jit(solution)/shard_map/ppermute | solution.py:250
  74.9 2.3 %collective-permute-start.4 = (bf16[1,256,256]{2,1,0:T(8,128)(2,1)S(1)}, bf16[1,256,256]{2,1,0:T(8,128)(2,1)S(1)}, u32[]{:S(2)}, u32[]{:S(2)}) collective-permute-start(bf16[1,256,256]{2,1,0:T(8,128)(2,1)S(1)} %get-tuple-element.24), channel_id=1, source_target_pairs={{0,8},{1,9},{2,10},{3,11},{4,12},{5,13},{6,14},{7,15},{8,16},{9,17... | collective-permute-start | bytes 393224 | tf_op jit(solution)/shard_map/ppermute | solution.py:250
  77.2 5.1 %collective-permute-start.5 = (bf16[1,256,256]{2,1,0:T(8,128)(2,1)S(1)}, bf16[1,256,256]{2,1,0:T(8,128)(2,1)S(1)}, u32[]{:S(2)}, u32[]{:S(2)}) collective-permute-start(bf16[1,256,256]{2,1,0:T(8,128)(2,1)S(1)} %get-tuple-element.25), channel_id=1, source_target_pairs={{0,24},{1,25},{2,26},{3,27},{4,28},{5,29},{6,30},{7,31},{8,0},{9,1... | collective-permute-start | bytes 393224 | tf_op jit(solution)/shard_map/ppermute | solution.py:250
  82.3 2.2 %column_terms.2 = (bf16[2,256,256]{2,1,0:T(8,128)(2,1)S(1)}, bf16[2,256,256]{2,1,0:T(8,128)(2,1)S(1)}, bf16[2,256,256]{2,1,0:T(8,128)(2,1)S(1)}) custom-call(s32[33]{0:T(128)S(1)} %copy-done.3, bf16[32,256,256]{2,1,0:T(8,128)(2,1)} %all-to-all-done.arrived), custom_call_target="tpu_custom_call" | custom-call | tf_op jit(solution)/shard_map/column_terms/pallas_call | solution.py:310
  86.5 3.5 %collective-permute-done.5.far_down = bf16[1,256,256]{2,1,0:T(8,128)(2,1)S(1)} collective-permute-done((bf16[1,256,256]{2,1,0:T(8,128)(2,1)S(1)}, bf16[1,256,256]{2,1,0:T(8,128)(2,1)S(1)}, u32[]{:S(2)}, u32[]{:S(2)}) %collective-permute-start.5) | collective-permute-done | bytes 131104 | tf_op jit(solution)/shard_map/ppermute | solution.py:250
  90.1 4.9 %collective-permute-start.6 = (bf16[2,256,256]{2,1,0:T(8,128)(2,1)S(1)}, bf16[2,256,256]{2,1,0:T(8,128)(2,1)S(1)}, u32[]{:S(2)}, u32[]{:S(2)}) collective-permute-start(bf16[2,256,256]{2,1,0:T(8,128)(2,1)S(1)} %get-tuple-element.28), channel_id=1, source_target_pairs={{0,8},{1,9},{2,10},{3,11},{4,12},{5,13},{6,14},{7,15},{8,16},{9,17... | collective-permute-start | bytes 786440 | tf_op jit(solution)/shard_map/ppermute | solution.py:250
  95.0 3.1 %collective-permute-start.7 = (bf16[2,256,256]{2,1,0:T(8,128)(2,1)S(1)}, bf16[2,256,256]{2,1,0:T(8,128)(2,1)S(1)}, u32[]{:S(2)}, u32[]{:S(2)}) collective-permute-start(bf16[2,256,256]{2,1,0:T(8,128)(2,1)S(1)} %get-tuple-element.29), channel_id=1, source_target_pairs={{0,24},{1,25},{2,26},{3,27},{4,28},{5,29},{6,30},{7,31},{8,0},{9,1... | collective-permute-start | bytes 786440 | tf_op jit(solution)/shard_map/ppermute | solution.py:250
  98.1 2.9 %edges.1.partial = f32[2,256,256]{2,1,0:T(8,128)} custom-call(s32[2,2]{1,0:T(2,128)} %edge_local.1, f32[2,2]{1,0:T(2,128)} %edge_coupling.1, f32[2]{0:T(128)} %gap.3, bf16[2,256,256]{2,1,0:T(8,128)(2,1)} %get-tuple-element.16.masked.rest_0_, bf16[2,256,256]{2,1,0:T(8,128)(2,1)} %integrals.1, f32[2,256]{1,0:T(2,128)} %virt.3, ...), custom_call_target="tpu_custom_call" | custom-call | tf_op jit(solution)/shard_map/edges/pallas_call | solution.py:348
  101.0 13.1 %all-to-all-done.1.rest_5_ = bf16[32,256,256]{2,1,0:T(8,128)(2,1)} async-done(((bf16[32,256,256]{2,1,0:T(8,128)(2,1)}), bf16[32,256,256]{2,1,0:T(8,128)(2,1)}, u32[]{:S(2)}, u32[]{:S(2)}) %all-to-all-start.1) | async-done | bytes 4194336 | tf_op jit(solution)/shard_map/all_to_all | solution.py:246
  115.0 5.6 %residual_update.1 = (f32[2,256,256]{2,1,0:T(8,128)}, bf16[2,256,256]{2,1,0:T(8,128)(2,1)}) custom-call(s32[64]{0:T(128)} %bucket.3, s32[8,64]{1,0:T(8,128)} %bitcast.3, f32[2,8]{1,0:T(2,128)} %coupling.3, f32[2]{0:T(128)} %gap.3, bf16[2,256,256]{2,1,0:T(8,128)(2,1)} %get-tuple-element.16.masked.rest_0_, f32[2,256,256]{2,1,0:T(8,128)} %edges.1.partial, ...), custom_call_target="tpu_custom_call" | custom-call | tf_op jit(solution)/shard_map/residual_update/pallas_call | solution.py:367
  (56 shorter events, 12.4 us)
Async XLA Ops:
  5.4 55.2 %all-to-all-start = ((bf16[32,256,256]{2,1,0:T(8,128)(2,1)}), bf16[32,256,256]{2,1,0:T(8,128)(2,1)}, u32[]{:S(2)}, u32[]{:S(2)}) async-start(bf16[32,256,256]{2,1,0:T(8,128)(2,1)} %get-tuple-element.20), calls=%async_computation | async-start | bytes 8388608 | tf_op jit(solution)/shard_map/all_to_all | solution.py:246
  10.4 20.7 %collective-permute-start.11 = (bf16[2,256,256]{2,1,0:T(8,128)(2,1)S(1)}, bf16[2,256,256]{2,1,0:T(8,128)(2,1)S(1)}, u32[]{:S(2)}, u32[]{:S(2)}) collective-permute-start(bf16[2,256,256]{2,1,0:T(8,128)(2,1)S(1)} %copy-done.4), channel_id=1, source_target_pairs={{0,8},{1,9},{2,10},{3,11},{4,12},{5,13},{6,14},{7,15},{8,16},{9,17... | collective-permute-start | bytes 786440 | tf_op jit(solution)/shard_map/ppermute | solution.py:250
  15.4 20.6 %collective-permute-start.10 = (bf16[2,256,256]{2,1,0:T(8,128)(2,1)S(1)}, bf16[2,256,256]{2,1,0:T(8,128)(2,1)S(1)}, u32[]{:S(2)}, u32[]{:S(2)}) collective-permute-start(bf16[2,256,256]{2,1,0:T(8,128)(2,1)S(1)} %copy-done.4), channel_id=1, source_target_pairs={{0,24},{1,25},{2,26},{3,27},{4,28},{5,29},{6,30},{7,31},{8,0},{9,1... | collective-permute-start | bytes 786440 | tf_op jit(solution)/shard_map/ppermute | solution.py:250
  19.0 18.9 %collective-permute-start.9 = (bf16[2,256,256]{2,1,0:T(8,128)(2,1)S(1)}, bf16[2,256,256]{2,1,0:T(8,128)(2,1)S(1)}, u32[]{:S(2)}, u32[]{:S(2)}) collective-permute-start(bf16[2,256,256]{2,1,0:T(8,128)(2,1)S(1)} %copy-done.4), channel_id=1, source_target_pairs={{0,4},{1,5},{2,6},{3,7},{4,8},{5,9},{6,10},{7,11},{8,12},{9,13},{1... | collective-permute-start | bytes 786440 | tf_op jit(solution)/shard_map/ppermute | solution.py:250
  21.8 20.7 %collective-permute-start.1 = (bf16[2,256,256]{2,1,0:T(8,128)(2,1)S(1)}, bf16[2,256,256]{2,1,0:T(8,128)(2,1)S(1)}, u32[]{:S(2)}, u32[]{:S(2)}) collective-permute-start(bf16[2,256,256]{2,1,0:T(8,128)(2,1)S(1)} %copy-done.4), channel_id=1, source_target_pairs={{32,0},{64,32},{96,64},{128,96},{160,128},{192,160},{224,192},{256... | collective-permute-start | bytes 786440 | tf_op jit(solution)/shard_map/ppermute | solution.py:287
  29.2 15.3 %collective-permute-start = (bf16[2,256,256]{2,1,0:T(8,128)(2,1)S(1)}, bf16[2,256,256]{2,1,0:T(8,128)(2,1)S(1)}, u32[]{:S(2)}, u32[]{:S(2)}) collective-permute-start(bf16[2,256,256]{2,1,0:T(8,128)(2,1)S(1)} %copy-done.4), channel_id=1, source_target_pairs={{0,32},{32,64},{64,96},{96,128},{128,160},{160,192},{192,224},{224... | collective-permute-start | bytes 786440 | tf_op jit(solution)/shard_map/ppermute | solution.py:286
  31.1 24.1 %copy-start.5 = (bf16[2,256,256]{2,1,0:T(8,128)(2,1)}, bf16[2,256,256]{2,1,0:T(8,128)(2,1)S(1)}, u32[]{:S(2)}) copy-start(bf16[2,256,256]{2,1,0:T(8,128)(2,1)S(1)} %collective-permute-done.11.rest_4_) | copy-start | bytes 786436
  31.1 20.4 %collective-permute-start.8 = (bf16[2,256,256]{2,1,0:T(8,128)(2,1)S(1)}, bf16[2,256,256]{2,1,0:T(8,128)(2,1)S(1)}, u32[]{:S(2)}, u32[]{:S(2)}) collective-permute-start(bf16[2,256,256]{2,1,0:T(8,128)(2,1)S(1)} %copy-done.4), channel_id=1, source_target_pairs={{0,28},{1,29},{2,30},{3,31},{4,0},{5,1},{6,2},{7,3},{8,4},{9,5},{1... | collective-permute-start | bytes 786440 | tf_op jit(solution)/shard_map/ppermute | solution.py:250
  36.0 19.3 %copy-start.6 = (bf16[2,256,256]{2,1,0:T(8,128)(2,1)}, bf16[2,256,256]{2,1,0:T(8,128)(2,1)S(1)}, u32[]{:S(2)}) copy-start(bf16[2,256,256]{2,1,0:T(8,128)(2,1)S(1)} %collective-permute-done.10.rest_3_) | copy-start | bytes 786436
  36.0 19.2 %collective-permute-start.13 = (bf16[2,256,256]{2,1,0:T(8,128)(2,1)S(1)}, bf16[2,256,256]{2,1,0:T(8,128)(2,1)S(1)}, u32[]{:S(2)}, u32[]{:S(2)}) collective-permute-start(bf16[2,256,256]{2,1,0:T(8,128)(2,1)S(1)} %collective-permute-done.11.rest_4_), channel_id=1, source_target_pairs={{0,4},{1,5},{2,6},{3,7},{4,8},{5,9},{6,10},{7,11},{8,12},{9,13},{1... | collective-permute-start | bytes 786440 | tf_op jit(solution)/shard_map/ppermute | solution.py:250
  37.9 17.3 %copy-start.9 = (bf16[2,256,256]{2,1,0:T(8,128)(2,1)}, bf16[2,256,256]{2,1,0:T(8,128)(2,1)S(1)}, u32[]{:S(2)}) copy-start(bf16[2,256,256]{2,1,0:T(8,128)(2,1)S(1)} %collective-permute-done.9.rest_2_) | copy-start | bytes 786436
  37.9 17.3 %collective-permute-start.12 = (bf16[2,256,256]{2,1,0:T(8,128)(2,1)S(1)}, bf16[2,256,256]{2,1,0:T(8,128)(2,1)S(1)}, u32[]{:S(2)}, u32[]{:S(2)}) collective-permute-start(bf16[2,256,256]{2,1,0:T(8,128)(2,1)S(1)} %collective-permute-done.10.rest_3_), channel_id=1, source_target_pairs={{0,28},{1,29},{2,30},{3,31},{4,0},{5,1},{6,2},{7,3},{8,4},{9,5},{1... | collective-permute-start | bytes 786440 | tf_op jit(solution)/shard_map/ppermute | solution.py:250
  42.6 18.1 %copy-start.7 = (bf16[2,256,256]{2,1,0:T(8,128)(2,1)}, bf16[2,256,256]{2,1,0:T(8,128)(2,1)S(1)}, u32[]{:S(2)}) copy-start(bf16[2,256,256]{2,1,0:T(8,128)(2,1)S(1)} %collective-permute-done.1.upper) | copy-start | bytes 786436
  42.6 11.7 %collective-permute-start.15 = (bf16[1,256,256]{2,1,0:T(8,128)(2,1)S(1)}, bf16[1,256,256]{2,1,0:T(8,128)(2,1)S(1)}, u32[]{:S(2)}, u32[]{:S(2)}) collective-permute-start(bf16[1,256,256]{2,1,0:T(8,128)(2,1)S(1)} %slice.9), channel_id=1, source_target_pairs={{0,8},{1,9},{2,10},{3,11},{4,12},{5,13},{6,14},{7,15},{8,16},{9,17... | collective-permute-start | bytes 393224 | tf_op jit(solution)/shard_map/ppermute | solution.py:250
  44.5 10.7 %collective-permute-start.14 = (bf16[1,256,256]{2,1,0:T(8,128)(2,1)S(1)}, bf16[1,256,256]{2,1,0:T(8,128)(2,1)S(1)}, u32[]{:S(2)}, u32[]{:S(2)}) collective-permute-start(bf16[1,256,256]{2,1,0:T(8,128)(2,1)S(1)} %slice.8), channel_id=1, source_target_pairs={{0,24},{1,25},{2,26},{3,27},{4,28},{5,29},{6,30},{7,31},{8,0},{9,1... | collective-permute-start | bytes 393224 | tf_op jit(solution)/shard_map/ppermute | solution.py:250
  60.7 53.5 %all-to-all-start.1 = ((bf16[32,256,256]{2,1,0:T(8,128)(2,1)}), bf16[32,256,256]{2,1,0:T(8,128)(2,1)}, u32[]{:S(2)}, u32[]{:S(2)}) async-start(bf16[32,256,256]{2,1,0:T(8,128)(2,1)} %named_pairs.1), calls=%async_computation.1 | async-start | bytes 8388608 | tf_op jit(solution)/shard_map/all_to_all | solution.py:246
  68.4 21.5 %collective-permute-start.2 = (bf16[4,256,256]{2,1,0:T(8,128)(2,1)S(1)}, bf16[4,256,256]{2,1,0:T(8,128)(2,1)S(1)}, u32[]{:S(2)}, u32[]{:S(2)}) collective-permute-start(bf16[4,256,256]{2,1,0:T(8,128)(2,1)S(1)} %get-tuple-element.22), channel_id=1, source_target_pairs={{0,4},{1,5},{2,6},{3,7},{4,8},{5,9},{6,10},{7,11},{8,12},{9,13},{1... | collective-permute-start | bytes 1572872 | tf_op jit(solution)/shard_map/ppermute | solution.py:250
  70.4 19.5 %collective-permute-start.3 = (bf16[4,256,256]{2,1,0:T(8,128)(2,1)S(1)}, bf16[4,256,256]{2,1,0:T(8,128)(2,1)S(1)}, u32[]{:S(2)}, u32[]{:S(2)}) collective-permute-start(bf16[4,256,256]{2,1,0:T(8,128)(2,1)S(1)} %get-tuple-element.23), channel_id=1, source_target_pairs={{0,28},{1,29},{2,30},{3,31},{4,0},{5,1},{6,2},{7,3},{8,4},{9,5},{1... | collective-permute-start | bytes 1572872 | tf_op jit(solution)/shard_map/ppermute | solution.py:250
  74.9 11.6 %collective-permute-start.4 = (bf16[1,256,256]{2,1,0:T(8,128)(2,1)S(1)}, bf16[1,256,256]{2,1,0:T(8,128)(2,1)S(1)}, u32[]{:S(2)}, u32[]{:S(2)}) collective-permute-start(bf16[1,256,256]{2,1,0:T(8,128)(2,1)S(1)} %get-tuple-element.24), channel_id=1, source_target_pairs={{0,8},{1,9},{2,10},{3,11},{4,12},{5,13},{6,14},{7,15},{8,16},{9,17... | collective-permute-start | bytes 393224 | tf_op jit(solution)/shard_map/ppermute | solution.py:250
  77.2 12.7 %collective-permute-start.5 = (bf16[1,256,256]{2,1,0:T(8,128)(2,1)S(1)}, bf16[1,256,256]{2,1,0:T(8,128)(2,1)S(1)}, u32[]{:S(2)}, u32[]{:S(2)}) collective-permute-start(bf16[1,256,256]{2,1,0:T(8,128)(2,1)S(1)} %get-tuple-element.25), channel_id=1, source_target_pairs={{0,24},{1,25},{2,26},{3,27},{4,28},{5,29},{6,30},{7,31},{8,0},{9,1... | collective-permute-start | bytes 393224 | tf_op jit(solution)/shard_map/ppermute | solution.py:250
  89.9 24.3 %copy-start = (bf16[4,256,256]{2,1,0:T(8,128)(2,1)}, bf16[4,256,256]{2,1,0:T(8,128)(2,1)S(1)}, u32[]{:S(2)}) copy-start(bf16[4,256,256]{2,1,0:T(8,128)(2,1)S(1)} %collective-permute-done.2.got_up.rest_1_) | copy-start | bytes 1572868
  89.9 24.3 %copy-start.1 = (bf16[4,256,256]{2,1,0:T(8,128)(2,1)}, bf16[4,256,256]{2,1,0:T(8,128)(2,1)S(1)}, u32[]{:S(2)}) copy-start(bf16[4,256,256]{2,1,0:T(8,128)(2,1)S(1)} %collective-permute-done.3.got_down.rest_2_) | copy-start | bytes 1572868
  90.1 24.1 %collective-permute-start.6 = (bf16[2,256,256]{2,1,0:T(8,128)(2,1)S(1)}, bf16[2,256,256]{2,1,0:T(8,128)(2,1)S(1)}, u32[]{:S(2)}, u32[]{:S(2)}) collective-permute-start(bf16[2,256,256]{2,1,0:T(8,128)(2,1)S(1)} %get-tuple-element.28), channel_id=1, source_target_pairs={{0,8},{1,9},{2,10},{3,11},{4,12},{5,13},{6,14},{7,15},{8,16},{9,17... | collective-permute-start | bytes 786440 | tf_op jit(solution)/shard_map/ppermute | solution.py:250
  95.0 19.1 %collective-permute-start.7 = (bf16[2,256,256]{2,1,0:T(8,128)(2,1)S(1)}, bf16[2,256,256]{2,1,0:T(8,128)(2,1)S(1)}, u32[]{:S(2)}, u32[]{:S(2)}) collective-permute-start(bf16[2,256,256]{2,1,0:T(8,128)(2,1)S(1)} %get-tuple-element.29), channel_id=1, source_target_pairs={{0,24},{1,25},{2,26},{3,27},{4,28},{5,29},{6,30},{7,31},{8,0},{9,1... | collective-permute-start | bytes 786440 | tf_op jit(solution)/shard_map/ppermute | solution.py:250
  (11 other events, 35.1 us)

commit v5 on v4

--- a/solution.py
+++ b/solution.py
@@ -60,7 +60,6 @@
     for entry in range(NBR):
         term = jnp.dot(halves[entry], inter[0, entry], preferred_element_type=F32)
         terms[pair * NBR + entry] = (coupling[pair, entry] * term).astype(BF)
-    for entry in range(NBR):
         copy(pair, entry).start()
 
     @pl.when(pair == 1)
@@ -195,8 +194,29 @@
     partial[0] = integrals[0].astype(F32) + gap_matrix(virt, gap, pair) * own - total
 
 
-def final_kernel(bucket, nbr, coupling, gap, masked, partial, virt, inter, *rest):
-    terms, (named, residual, new_amps, partners, sems) = rest[:-5], rest[-5:]
+def gather_kernel(partial, *rest):
+    terms, out = rest[:-1], rest[-1]
+    total = partial[0]
+    for ref in terms:
+        total -= ref[0].astype(F32)
+    out[0] = total
+
+
+def final_kernel(
+    bucket,
+    nbr,
+    coupling,
+    gap,
+    masked,
+    partial,
+    virt,
+    inter,
+    named,
+    residual,
+    new_amps,
+    partners,
+    sems,
+):
     dev, _, _ = place()
     pair = pl.program_id(0)
 
@@ -212,13 +232,16 @@
     for entry in range(NBR):
         partner_copy(pair * NBR + entry, entry).wait()
 
-    total = terms[0][0].astype(F32)
-    for ref in terms[1:]:
-        total += ref[0].astype(F32)
+    halves = []
     for entry in range(NBR):
-        total += coupling[pair, entry] * project(inter[0, entry], partners[pair * NBR + entry])
+        partner = partners[pair * NBR + entry]
+        half = jnp.dot(inter[0, entry], partner, preferred_element_type=F32)
+        halves.append(half.astype(BF))
+    total = partial[0]
+    for entry in range(NBR):
+        total -= coupling[pair, entry] * times_transposed(halves[entry], inter[0, entry])
     keep = keep_square(jnp.left_shift(32, bucket[2 * dev + pair]))
-    value = jnp.where(keep, partial[0] - total, 0.0)
+    value = jnp.where(keep, total, 0.0)
     residual[0] = value
     change = value / gap_matrix(virt, gap, pair)
     new_amps[0] = jnp.where(keep, masked[0].astype(F32) - change, 0.0).astype(BF)
@@ -364,10 +387,19 @@
         lower,
         upper,
     )
+    partial = pl.pallas_call(
+        gather_kernel,
+        grid=(2,),
+        in_specs=[each] * (1 + len(terms)),
+        out_specs=each,
+        out_shape=jax.ShapeDtypeStruct((2, R, R), F32),
+        compiler_params=pltpu.CompilerParams(vmem_limit_bytes=12 << 20),
+        name="gathered_terms",
+    )(partial, *terms)
     outputs = pl.pallas_call(
         final_kernel,
         grid=(2,),
-        in_specs=[SMEM] * 4 + [each, each, VMEM, each_of(NBR)] + [each] * len(terms) + [ANY],
+        in_specs=[SMEM] * 4 + [each, each, VMEM, each_of(NBR)] + [ANY],
         out_specs=[each, each],
         out_shape=[
             jax.ShapeDtypeStruct((2, R, R), F32),
@@ -388,7 +420,6 @@
         partial,
         virt_energy,
         intersection,
-        *terms,
         named,
     )
     return tuple(outputs)

time: 123 us -> 121 us (0.984)
    all_to_all x2, waiting for transfers between devices: 13.1 us -> 5.94 us  [swap_columns(): lax.all_to_all(value, 'dev', 0, 0, tiled=True, axis_index_groups=rows)]
    ppermute x14, waiting for transfers between devices: 8.38 us -> 15.1 us  [along_y(): return lax.ppermute(value, 'dev', perm)]
    unnamed x34 -> x28, local copies, waits for them, and re-layouts: 2.92 us -> 3.27 us
  transfers between devices with their start and end apart: 18 -> 18, of which waited for: 5 -> 6; matrix products, arithmetic and copies ran while one was open for 0% -> 0% of each run, Pallas kernels for 11% -> 11%
where the time goes in v5:
time: 121 us; the launch traced here: 119 us
  starting transfers between devices  70.8 us (59%)
  Pallas kernels  23.2 us (19%)
  waiting for transfers between devices  21 us (17%)
  local copies, waits for them, and re-layouts  3.29 us (3%)
    ppermute x14, starting transfers between devices, along_y(): return lax.ppermute(value, 'dev', perm)  51.8 us
    ppermute x14, waiting for transfers between devices, along_y(): return lax.ppermute(value, 'dev', perm)  15.1 us
    all_to_all x2, starting transfers between devices, swap_columns(): lax.all_to_all(value, 'dev', 0, 0, tiled=True, axis_index_groups=rows)  9.89 us
    ppermute x1, starting transfers between devices, local(): upper = lax.ppermute(masked, 'grp', [(i + 1, i) for i in range(groups - 1)])  7.19 us
    all_to_all x2, waiting for transfers between devices, swap_columns(): lax.all_to_all(value, 'dev', 0, 0, tiled=True, axis_index_groups=rows)  5.94 us
    pallas_call x1, Pallas kernels, local(): pl.pallas_call(final_kernel, grid=(2,), in_specs=[SMEM] * 4 + [each, each...  5.13 us
    pallas_call x2, Pallas kernels, column_terms(): pl.pallas_call(functools.partial(combine_kernel, groups), in_specs=[SMEM,...  4.93 us
    pallas_call x1, Pallas kernels, local(): pl.pallas_call(return_kernel, grid=(2,), in_specs=[SMEM, SMEM, SMEM, pl.B...  4.47 us
  transfers between devices with their start and end apart: 18, of which 6 were waited for; matrix products, arithmetic and copies ran while one was open for 0% of the time, Pallas kernels for 11%

profile of v5, /device:TPU:1, one launch (start us, length us, event | category | flops | bytes accessed | tf_op | source)
XLA Modules:
  0.0 119.3 jit_solution(11180283405660456077)
XLA Ops:
  0.6 4.5 %returned_terms.1 = (bf16[2,256,256]{2,1,0:T(8,128)(2,1)}, bf16[32,256,256]{2,1,0:T(8,128)(2,1)}) custom-call(s32[64]{0:T(128)} %bucket.3, s32[8,64]{1,0:T(8,128)} %bitcast.1, f32[2,8]{1,0:T(2,128)} %coupling.3, bf16[2,256,256]{2,1,0:T(8,128)(2,1)} %amps.1, bf16[2,8,256,256]{3,2,1,0:T(8,128)(2,1)} %inter.3), custom_call_target="tpu_custom_call" | custom-call | tf_op jit(solution)/shard_map/returned_terms/pallas_call | solution.py:276
  5.1 5.0 %all-to-all-start = ((bf16[32,256,256]{2,1,0:T(8,128)(2,1)}), bf16[32,256,256]{2,1,0:T(8,128)(2,1)}, u32[]{:S(2)}, u32[]{:S(2)}) async-start(bf16[32,256,256]{2,1,0:T(8,128)(2,1)} %get-tuple-element.20), calls=%async_computation | async-start | bytes 8388608 | tf_op jit(solution)/shard_map/all_to_all | solution.py:269
  10.1 5.1 %collective-permute-start.11 = (bf16[2,256,256]{2,1,0:T(8,128)(2,1)S(1)}, bf16[2,256,256]{2,1,0:T(8,128)(2,1)S(1)}, u32[]{:S(2)}, u32[]{:S(2)}) collective-permute-start(bf16[2,256,256]{2,1,0:T(8,128)(2,1)S(1)} %copy-done.3), channel_id=1, source_target_pairs={{0,8},{1,9},{2,10},{3,11},{4,12},{5,13},{6,14},{7,15},{8,16},{9,17... | collective-permute-start | bytes 786440 | tf_op jit(solution)/shard_map/ppermute | solution.py:273
  15.2 3.6 %collective-permute-start.10 = (bf16[2,256,256]{2,1,0:T(8,128)(2,1)S(1)}, bf16[2,256,256]{2,1,0:T(8,128)(2,1)S(1)}, u32[]{:S(2)}, u32[]{:S(2)}) collective-permute-start(bf16[2,256,256]{2,1,0:T(8,128)(2,1)S(1)} %copy-done.3), channel_id=1, source_target_pairs={{0,24},{1,25},{2,26},{3,27},{4,28},{5,29},{6,30},{7,31},{8,0},{9,1... | collective-permute-start | bytes 786440 | tf_op jit(solution)/shard_map/ppermute | solution.py:273
  18.8 2.8 %collective-permute-start.9 = (bf16[2,256,256]{2,1,0:T(8,128)(2,1)S(1)}, bf16[2,256,256]{2,1,0:T(8,128)(2,1)S(1)}, u32[]{:S(2)}, u32[]{:S(2)}) collective-permute-start(bf16[2,256,256]{2,1,0:T(8,128)(2,1)S(1)} %copy-done.3), channel_id=1, source_target_pairs={{0,4},{1,5},{2,6},{3,7},{4,8},{5,9},{6,10},{7,11},{8,12},{9,13},{1... | collective-permute-start | bytes 786440 | tf_op jit(solution)/shard_map/ppermute | solution.py:273
  21.6 7.2 %collective-permute-start.1 = (bf16[2,256,256]{2,1,0:T(8,128)(2,1)S(1)}, bf16[2,256,256]{2,1,0:T(8,128)(2,1)S(1)}, u32[]{:S(2)}, u32[]{:S(2)}) collective-permute-start(bf16[2,256,256]{2,1,0:T(8,128)(2,1)S(1)} %copy-done.3), channel_id=1, source_target_pairs={{32,0},{64,32},{96,64},{128,96},{160,128},{192,160},{224,192},{256... | collective-permute-start | bytes 786440 | tf_op jit(solution)/shard_map/ppermute | solution.py:310
  30.8 4.9 %collective-permute-start.8 = (bf16[2,256,256]{2,1,0:T(8,128)(2,1)S(1)}, bf16[2,256,256]{2,1,0:T(8,128)(2,1)S(1)}, u32[]{:S(2)}, u32[]{:S(2)}) collective-permute-start(bf16[2,256,256]{2,1,0:T(8,128)(2,1)S(1)} %copy-done.3), channel_id=1, source_target_pairs={{0,28},{1,29},{2,30},{3,31},{4,0},{5,1},{6,2},{7,3},{8,4},{9,5},{1... | collective-permute-start | bytes 786440 | tf_op jit(solution)/shard_map/ppermute | solution.py:273
  37.6 4.6 %collective-permute-start.12 = (bf16[2,256,256]{2,1,0:T(8,128)(2,1)S(1)}, bf16[2,256,256]{2,1,0:T(8,128)(2,1)S(1)}, u32[]{:S(2)}, u32[]{:S(2)}) collective-permute-start(bf16[2,256,256]{2,1,0:T(8,128)(2,1)S(1)} %collective-permute-done.10.rest_3_), channel_id=1, source_target_pairs={{0,28},{1,29},{2,30},{3,31},{4,0},{5,1},{6,2},{7,3},{8,4},{9,5},{1... | collective-permute-start | bytes 786440 | tf_op jit(solution)/shard_map/ppermute | solution.py:273
  44.2 5.5 %collective-permute-start.14 = (bf16[1,256,256]{2,1,0:T(8,128)(2,1)S(1)}, bf16[1,256,256]{2,1,0:T(8,128)(2,1)S(1)}, u32[]{:S(2)}, u32[]{:S(2)}) collective-permute-start(bf16[1,256,256]{2,1,0:T(8,128)(2,1)S(1)} %slice.8), channel_id=1, source_target_pairs={{0,24},{1,25},{2,26},{3,27},{4,28},{5,29},{6,30},{7,31},{8,0},{9,1... | collective-permute-start | bytes 393224 | tf_op jit(solution)/shard_map/ppermute | solution.py:273
  51.2 2.7 %collective-permute-done.15.rest_8_ = bf16[1,256,256]{2,1,0:T(8,128)(2,1)S(1)} collective-permute-done((bf16[1,256,256]{2,1,0:T(8,128)(2,1)S(1)}, bf16[1,256,256]{2,1,0:T(8,128)(2,1)S(1)}, u32[]{:S(2)}, u32[]{:S(2)}) %collective-permute-start.15) | collective-permute-done | bytes 131104 | tf_op jit(solution)/shard_map/ppermute | solution.py:273
  56.4 3.9 %named_pairs.1 = bf16[32,256,256]{2,1,0:T(8,128)(2,1)} custom-call(s32[33]{0:T(128)} %served_pairs.1.served, bf16[2,256,256]{2,1,0:T(8,128)(2,1)} %get-tuple-element.16.masked.rest_0_, bf16[2,256,256]{2,1,0:T(8,128)(2,1)} %copy-done.9, bf16[2,256,256]{2,1,0:T(8,128)(2,1)} %copy-done.8, bf16[2,256,256]{2,1,0:T(8,128)(2,1)} %copy-done.5, ...), custom_call_target="tpu_custom_call" | custom-call | tf_op jit(solution)/shard_map/named_pairs/pallas_call | solution.py:312
  60.3 4.9 %all-to-all-start.1 = ((bf16[32,256,256]{2,1,0:T(8,128)(2,1)}), bf16[32,256,256]{2,1,0:T(8,128)(2,1)}, u32[]{:S(2)}, u32[]{:S(2)}) async-start(bf16[32,256,256]{2,1,0:T(8,128)(2,1)} %named_pairs.1), calls=%async_computation.1 | async-start | bytes 8388608 | tf_op jit(solution)/shard_map/all_to_all | solution.py:269
  65.3 2.6 %column_terms.3 = (bf16[4,256,256]{2,1,0:T(8,128)(2,1)S(1)}, bf16[4,256,256]{2,1,0:T(8,128)(2,1)S(1)}, bf16[1,256,256]{2,1,0:T(8,128)(2,1)S(1)}, bf16[1,256,256]{2,1,0:T(8,128)(2,1)S(1)}) custom-call(s32[33]{0:T(128)S(1)} %copy-done.2, bf16[32,256,256]{2,1,0:T(8,128)(2,1)} %all-to-all-done.arrived), custom_call_target="tpu_custom_call" | custom-call | tf_op jit(solution)/shard_map/column_terms/pallas_call | solution.py:333
  67.9 2.3 %collective-permute-start.2 = (bf16[4,256,256]{2,1,0:T(8,128)(2,1)S(1)}, bf16[4,256,256]{2,1,0:T(8,128)(2,1)S(1)}, u32[]{:S(2)}, u32[]{:S(2)}) collective-permute-start(bf16[4,256,256]{2,1,0:T(8,128)(2,1)S(1)} %get-tuple-element.22), channel_id=1, source_target_pairs={{0,4},{1,5},{2,6},{3,7},{4,8},{5,9},{6,10},{7,11},{8,12},{9,13},{1... | collective-permute-start | bytes 1572872 | tf_op jit(solution)/shard_map/ppermute | solution.py:273
  70.2 4.2 %collective-permute-start.3 = (bf16[4,256,256]{2,1,0:T(8,128)(2,1)S(1)}, bf16[4,256,256]{2,1,0:T(8,128)(2,1)S(1)}, u32[]{:S(2)}, u32[]{:S(2)}) collective-permute-start(bf16[4,256,256]{2,1,0:T(8,128)(2,1)S(1)} %get-tuple-element.23), channel_id=1, source_target_pairs={{0,28},{1,29},{2,30},{3,31},{4,0},{5,1},{6,2},{7,3},{8,4},{9,5},{1... | collective-permute-start | bytes 1572872 | tf_op jit(solution)/shard_map/ppermute | solution.py:273
  74.4 2.4 %collective-permute-start.4 = (bf16[1,256,256]{2,1,0:T(8,128)(2,1)S(1)}, bf16[1,256,256]{2,1,0:T(8,128)(2,1)S(1)}, u32[]{:S(2)}, u32[]{:S(2)}) collective-permute-start(bf16[1,256,256]{2,1,0:T(8,128)(2,1)S(1)} %get-tuple-element.24), channel_id=1, source_target_pairs={{0,8},{1,9},{2,10},{3,11},{4,12},{5,13},{6,14},{7,15},{8,16},{9,17... | collective-permute-start | bytes 393224 | tf_op jit(solution)/shard_map/ppermute | solution.py:273
  76.9 4.9 %collective-permute-start.5 = (bf16[1,256,256]{2,1,0:T(8,128)(2,1)S(1)}, bf16[1,256,256]{2,1,0:T(8,128)(2,1)S(1)}, u32[]{:S(2)}, u32[]{:S(2)}) collective-permute-start(bf16[1,256,256]{2,1,0:T(8,128)(2,1)S(1)} %get-tuple-element.25), channel_id=1, source_target_pairs={{0,24},{1,25},{2,26},{3,27},{4,28},{5,29},{6,30},{7,31},{8,0},{9,1... | collective-permute-start | bytes 393224 | tf_op jit(solution)/shard_map/ppermute | solution.py:273
  81.8 2.3 %column_terms.2 = (bf16[2,256,256]{2,1,0:T(8,128)(2,1)S(1)}, bf16[2,256,256]{2,1,0:T(8,128)(2,1)S(1)}, bf16[2,256,256]{2,1,0:T(8,128)(2,1)S(1)}) custom-call(s32[33]{0:T(128)S(1)} %copy-done.2, bf16[32,256,256]{2,1,0:T(8,128)(2,1)} %all-to-all-done.arrived), custom_call_target="tpu_custom_call" | custom-call | tf_op jit(solution)/shard_map/column_terms/pallas_call | solution.py:333
  86.3 3.2 %collective-permute-done.5.far_down = bf16[1,256,256]{2,1,0:T(8,128)(2,1)S(1)} collective-permute-done((bf16[1,256,256]{2,1,0:T(8,128)(2,1)S(1)}, bf16[1,256,256]{2,1,0:T(8,128)(2,1)S(1)}, u32[]{:S(2)}, u32[]{:S(2)}) %collective-permute-start.5) | collective-permute-done | bytes 131104 | tf_op jit(solution)/shard_map/ppermute | solution.py:273
  89.6 5.7 %collective-permute-start.6 = (bf16[2,256,256]{2,1,0:T(8,128)(2,1)S(1)}, bf16[2,256,256]{2,1,0:T(8,128)(2,1)S(1)}, u32[]{:S(2)}, u32[]{:S(2)}) collective-permute-start(bf16[2,256,256]{2,1,0:T(8,128)(2,1)S(1)} %get-tuple-element.28), channel_id=1, source_target_pairs={{0,8},{1,9},{2,10},{3,11},{4,12},{5,13},{6,14},{7,15},{8,16},{9,17... | collective-permute-start | bytes 786440 | tf_op jit(solution)/shard_map/ppermute | solution.py:273
  97.4 2.9 %edges.1.partial = f32[2,256,256]{2,1,0:T(8,128)} custom-call(s32[2,2]{1,0:T(2,128)} %edge_local.1, f32[2,2]{1,0:T(2,128)} %edge_coupling.1, f32[2]{0:T(128)} %gap.3, bf16[2,256,256]{2,1,0:T(8,128)(2,1)} %get-tuple-element.16.masked.rest_0_, bf16[2,256,256]{2,1,0:T(8,128)(2,1)} %integrals.1, f32[2,256]{1,0:T(2,128)} %virt.3, ...), custom_call_target="tpu_custom_call" | custom-call | tf_op jit(solution)/shard_map/edges/pallas_call | solution.py:371
  100.3 5.9 %collective-permute-done.6.rest_3_ = bf16[2,256,256]{2,1,0:T(8,128)(2,1)S(1)} collective-permute-done((bf16[2,256,256]{2,1,0:T(8,128)(2,1)S(1)}, bf16[2,256,256]{2,1,0:T(8,128)(2,1)S(1)}, u32[]{:S(2)}, u32[]{:S(2)}) %collective-permute-start.6) | collective-permute-done | bytes 262176 | tf_op jit(solution)/shard_map/ppermute | solution.py:273
  108.2 5.9 %all-to-all-done.1.named = bf16[32,256,256]{2,1,0:T(8,128)(2,1)} async-done(((bf16[32,256,256]{2,1,0:T(8,128)(2,1)}), bf16[32,256,256]{2,1,0:T(8,128)(2,1)}, u32[]{:S(2)}, u32[]{:S(2)}) %all-to-all-start.1) | async-done | bytes 4194336 | tf_op jit(solution)/shard_map/all_to_all | solution.py:269
  114.2 5.1 %residual_update.1 = (f32[2,256,256]{2,1,0:T(8,128)}, bf16[2,256,256]{2,1,0:T(8,128)(2,1)}) custom-call(s32[64]{0:T(128)} %bucket.3, s32[8,64]{1,0:T(8,128)} %bitcast.3, f32[2,8]{1,0:T(2,128)} %coupling.3, f32[2]{0:T(128)} %gap.3, bf16[2,256,256]{2,1,0:T(8,128)(2,1)} %get-tuple-element.16.masked.rest_0_, f32[2,256,256]{2,1,0:T(8,128)} %copy-done.1, ...), custom_call_target="tpu_custom_call" | custom-call | tf_op jit(solution)/shard_map/residual_update/pallas_call | solution.py:399
  (51 shorter events, 16.1 us)
Async XLA Ops:
  5.1 5.0 %copy-start.3 = (bf16[2,256,256]{2,1,0:T(8,128)(2,1)S(1)}, bf16[2,256,256]{2,1,0:T(8,128)(2,1)}, u32[]{:S(2)}) copy-start(bf16[2,256,256]{2,1,0:T(8,128)(2,1)} %get-tuple-element.16.masked.rest_0_) | copy-start | bytes 786436
  5.1 55.2 %all-to-all-start = ((bf16[32,256,256]{2,1,0:T(8,128)(2,1)}), bf16[32,256,256]{2,1,0:T(8,128)(2,1)}, u32[]{:S(2)}, u32[]{:S(2)}) async-start(bf16[32,256,256]{2,1,0:T(8,128)(2,1)} %get-tuple-element.20), calls=%async_computation | async-start | bytes 8388608 | tf_op jit(solution)/shard_map/all_to_all | solution.py:269
  10.1 20.6 %collective-permute-start.11 = (bf16[2,256,256]{2,1,0:T(8,128)(2,1)S(1)}, bf16[2,256,256]{2,1,0:T(8,128)(2,1)S(1)}, u32[]{:S(2)}, u32[]{:S(2)}) collective-permute-start(bf16[2,256,256]{2,1,0:T(8,128)(2,1)S(1)} %copy-done.3), channel_id=1, source_target_pairs={{0,8},{1,9},{2,10},{3,11},{4,12},{5,13},{6,14},{7,15},{8,16},{9,17... | collective-permute-start | bytes 786440 | tf_op jit(solution)/shard_map/ppermute | solution.py:273
  15.2 20.4 %collective-permute-start.10 = (bf16[2,256,256]{2,1,0:T(8,128)(2,1)S(1)}, bf16[2,256,256]{2,1,0:T(8,128)(2,1)S(1)}, u32[]{:S(2)}, u32[]{:S(2)}) collective-permute-start(bf16[2,256,256]{2,1,0:T(8,128)(2,1)S(1)} %copy-done.3), channel_id=1, source_target_pairs={{0,24},{1,25},{2,26},{3,27},{4,28},{5,29},{6,30},{7,31},{8,0},{9,1... | collective-permute-start | bytes 786440 | tf_op jit(solution)/shard_map/ppermute | solution.py:273
  18.8 18.8 %collective-permute-start.9 = (bf16[2,256,256]{2,1,0:T(8,128)(2,1)S(1)}, bf16[2,256,256]{2,1,0:T(8,128)(2,1)S(1)}, u32[]{:S(2)}, u32[]{:S(2)}) collective-permute-start(bf16[2,256,256]{2,1,0:T(8,128)(2,1)S(1)} %copy-done.3), channel_id=1, source_target_pairs={{0,4},{1,5},{2,6},{3,7},{4,8},{5,9},{6,10},{7,11},{8,12},{9,13},{1... | collective-permute-start | bytes 786440 | tf_op jit(solution)/shard_map/ppermute | solution.py:273
  21.6 20.6 %collective-permute-start.1 = (bf16[2,256,256]{2,1,0:T(8,128)(2,1)S(1)}, bf16[2,256,256]{2,1,0:T(8,128)(2,1)S(1)}, u32[]{:S(2)}, u32[]{:S(2)}) collective-permute-start(bf16[2,256,256]{2,1,0:T(8,128)(2,1)S(1)} %copy-done.3), channel_id=1, source_target_pairs={{32,0},{64,32},{96,64},{128,96},{160,128},{192,160},{224,192},{256... | collective-permute-start | bytes 786440 | tf_op jit(solution)/shard_map/ppermute | solution.py:310
  28.8 15.3 %collective-permute-start = (bf16[2,256,256]{2,1,0:T(8,128)(2,1)S(1)}, bf16[2,256,256]{2,1,0:T(8,128)(2,1)S(1)}, u32[]{:S(2)}, u32[]{:S(2)}) collective-permute-start(bf16[2,256,256]{2,1,0:T(8,128)(2,1)S(1)} %copy-done.3), channel_id=1, source_target_pairs={{0,32},{32,64},{64,96},{96,128},{128,160},{160,192},{192,224},{224... | collective-permute-start | bytes 786440 | tf_op jit(solution)/shard_map/ppermute | solution.py:309
  30.8 24.2 %copy-start.4 = (bf16[2,256,256]{2,1,0:T(8,128)(2,1)}, bf16[2,256,256]{2,1,0:T(8,128)(2,1)S(1)}, u32[]{:S(2)}) copy-start(bf16[2,256,256]{2,1,0:T(8,128)(2,1)S(1)} %collective-permute-done.11.rest_4_) | copy-start | bytes 786436
  30.8 20.4 %collective-permute-start.8 = (bf16[2,256,256]{2,1,0:T(8,128)(2,1)S(1)}, bf16[2,256,256]{2,1,0:T(8,128)(2,1)S(1)}, u32[]{:S(2)}, u32[]{:S(2)}) collective-permute-start(bf16[2,256,256]{2,1,0:T(8,128)(2,1)S(1)} %copy-done.3), channel_id=1, source_target_pairs={{0,28},{1,29},{2,30},{3,31},{4,0},{5,1},{6,2},{7,3},{8,4},{9,5},{1... | collective-permute-start | bytes 786440 | tf_op jit(solution)/shard_map/ppermute | solution.py:273
  35.6 19.4 %copy-start.5 = (bf16[2,256,256]{2,1,0:T(8,128)(2,1)}, bf16[2,256,256]{2,1,0:T(8,128)(2,1)S(1)}, u32[]{:S(2)}) copy-start(bf16[2,256,256]{2,1,0:T(8,128)(2,1)S(1)} %collective-permute-done.10.rest_3_) | copy-start | bytes 786436
  35.6 19.3 %collective-permute-start.13 = (bf16[2,256,256]{2,1,0:T(8,128)(2,1)S(1)}, bf16[2,256,256]{2,1,0:T(8,128)(2,1)S(1)}, u32[]{:S(2)}, u32[]{:S(2)}) collective-permute-start(bf16[2,256,256]{2,1,0:T(8,128)(2,1)S(1)} %collective-permute-done.11.rest_4_), channel_id=1, source_target_pairs={{0,4},{1,5},{2,6},{3,7},{4,8},{5,9},{6,10},{7,11},{8,12},{9,13},{1... | collective-permute-start | bytes 786440 | tf_op jit(solution)/shard_map/ppermute | solution.py:273
  37.6 17.4 %copy-start.8 = (bf16[2,256,256]{2,1,0:T(8,128)(2,1)}, bf16[2,256,256]{2,1,0:T(8,128)(2,1)S(1)}, u32[]{:S(2)}) copy-start(bf16[2,256,256]{2,1,0:T(8,128)(2,1)S(1)} %collective-permute-done.9.rest_2_) | copy-start | bytes 786436
  37.6 17.4 %collective-permute-start.12 = (bf16[2,256,256]{2,1,0:T(8,128)(2,1)S(1)}, bf16[2,256,256]{2,1,0:T(8,128)(2,1)S(1)}, u32[]{:S(2)}, u32[]{:S(2)}) collective-permute-start(bf16[2,256,256]{2,1,0:T(8,128)(2,1)S(1)} %collective-permute-done.10.rest_3_), channel_id=1, source_target_pairs={{0,28},{1,29},{2,30},{3,31},{4,0},{5,1},{6,2},{7,3},{8,4},{9,5},{1... | collective-permute-start | bytes 786440 | tf_op jit(solution)/shard_map/ppermute | solution.py:273
  42.2 18.1 %copy-start.6 = (bf16[2,256,256]{2,1,0:T(8,128)(2,1)}, bf16[2,256,256]{2,1,0:T(8,128)(2,1)S(1)}, u32[]{:S(2)}) copy-start(bf16[2,256,256]{2,1,0:T(8,128)(2,1)S(1)} %collective-permute-done.1.upper) | copy-start | bytes 786436
  42.2 11.6 %collective-permute-start.15 = (bf16[1,256,256]{2,1,0:T(8,128)(2,1)S(1)}, bf16[1,256,256]{2,1,0:T(8,128)(2,1)S(1)}, u32[]{:S(2)}, u32[]{:S(2)}) collective-permute-start(bf16[1,256,256]{2,1,0:T(8,128)(2,1)S(1)} %slice.9), channel_id=1, source_target_pairs={{0,8},{1,9},{2,10},{3,11},{4,12},{5,13},{6,14},{7,15},{8,16},{9,17... | collective-permute-start | bytes 393224 | tf_op jit(solution)/shard_map/ppermute | solution.py:273
  44.2 16.2 %copy-start.7 = (bf16[2,256,256]{2,1,0:T(8,128)(2,1)}, bf16[2,256,256]{2,1,0:T(8,128)(2,1)S(1)}, u32[]{:S(2)}) copy-start(bf16[2,256,256]{2,1,0:T(8,128)(2,1)S(1)} %collective-permute-done.lower) | copy-start | bytes 786436
  44.2 10.8 %collective-permute-start.14 = (bf16[1,256,256]{2,1,0:T(8,128)(2,1)S(1)}, bf16[1,256,256]{2,1,0:T(8,128)(2,1)S(1)}, u32[]{:S(2)}, u32[]{:S(2)}) collective-permute-start(bf16[1,256,256]{2,1,0:T(8,128)(2,1)S(1)} %slice.8), channel_id=1, source_target_pairs={{0,24},{1,25},{2,26},{3,27},{4,28},{5,29},{6,30},{7,31},{8,0},{9,1... | collective-permute-start | bytes 393224 | tf_op jit(solution)/shard_map/ppermute | solution.py:273
  60.3 53.8 %all-to-all-start.1 = ((bf16[32,256,256]{2,1,0:T(8,128)(2,1)}), bf16[32,256,256]{2,1,0:T(8,128)(2,1)}, u32[]{:S(2)}, u32[]{:S(2)}) async-start(bf16[32,256,256]{2,1,0:T(8,128)(2,1)} %named_pairs.1), calls=%async_computation.1 | async-start | bytes 8388608 | tf_op jit(solution)/shard_map/all_to_all | solution.py:269
  67.9 21.5 %collective-permute-start.2 = (bf16[4,256,256]{2,1,0:T(8,128)(2,1)S(1)}, bf16[4,256,256]{2,1,0:T(8,128)(2,1)S(1)}, u32[]{:S(2)}, u32[]{:S(2)}) collective-permute-start(bf16[4,256,256]{2,1,0:T(8,128)(2,1)S(1)} %get-tuple-element.22), channel_id=1, source_target_pairs={{0,4},{1,5},{2,6},{3,7},{4,8},{5,9},{6,10},{7,11},{8,12},{9,13},{1... | collective-permute-start | bytes 1572872 | tf_op jit(solution)/shard_map/ppermute | solution.py:273
  70.2 19.2 %collective-permute-start.3 = (bf16[4,256,256]{2,1,0:T(8,128)(2,1)S(1)}, bf16[4,256,256]{2,1,0:T(8,128)(2,1)S(1)}, u32[]{:S(2)}, u32[]{:S(2)}) collective-permute-start(bf16[4,256,256]{2,1,0:T(8,128)(2,1)S(1)} %get-tuple-element.23), channel_id=1, source_target_pairs={{0,28},{1,29},{2,30},{3,31},{4,0},{5,1},{6,2},{7,3},{8,4},{9,5},{1... | collective-permute-start | bytes 1572872 | tf_op jit(solution)/shard_map/ppermute | solution.py:273
  74.4 11.9 %collective-permute-start.4 = (bf16[1,256,256]{2,1,0:T(8,128)(2,1)S(1)}, bf16[1,256,256]{2,1,0:T(8,128)(2,1)S(1)}, u32[]{:S(2)}, u32[]{:S(2)}) collective-permute-start(bf16[1,256,256]{2,1,0:T(8,128)(2,1)S(1)} %get-tuple-element.24), channel_id=1, source_target_pairs={{0,8},{1,9},{2,10},{3,11},{4,12},{5,13},{6,14},{7,15},{8,16},{9,17... | collective-permute-start | bytes 393224 | tf_op jit(solution)/shard_map/ppermute | solution.py:273
  76.9 12.6 %collective-permute-start.5 = (bf16[1,256,256]{2,1,0:T(8,128)(2,1)S(1)}, bf16[1,256,256]{2,1,0:T(8,128)(2,1)S(1)}, u32[]{:S(2)}, u32[]{:S(2)}) collective-permute-start(bf16[1,256,256]{2,1,0:T(8,128)(2,1)S(1)} %get-tuple-element.25), channel_id=1, source_target_pairs={{0,24},{1,25},{2,26},{3,27},{4,28},{5,29},{6,30},{7,31},{8,0},{9,1... | collective-permute-start | bytes 393224 | tf_op jit(solution)/shard_map/ppermute | solution.py:273
  89.6 16.6 %collective-permute-start.6 = (bf16[2,256,256]{2,1,0:T(8,128)(2,1)S(1)}, bf16[2,256,256]{2,1,0:T(8,128)(2,1)S(1)}, u32[]{:S(2)}, u32[]{:S(2)}) collective-permute-start(bf16[2,256,256]{2,1,0:T(8,128)(2,1)S(1)} %get-tuple-element.28), channel_id=1, source_target_pairs={{0,8},{1,9},{2,10},{3,11},{4,12},{5,13},{6,14},{7,15},{8,16},{9,17... | collective-permute-start | bytes 786440 | tf_op jit(solution)/shard_map/ppermute | solution.py:273
  95.3 10.9 %collective-permute-start.7 = (bf16[2,256,256]{2,1,0:T(8,128)(2,1)S(1)}, bf16[2,256,256]{2,1,0:T(8,128)(2,1)S(1)}, u32[]{:S(2)}, u32[]{:S(2)}) collective-permute-start(bf16[2,256,256]{2,1,0:T(8,128)(2,1)S(1)} %get-tuple-element.29), channel_id=1, source_target_pairs={{0,24},{1,25},{2,26},{3,27},{4,28},{5,29},{6,30},{7,31},{8,0},{9,1... | collective-permute-start | bytes 786440 | tf_op jit(solution)/shard_map/ppermute | solution.py:273
  (8 other events, 13.9 us)
